TPU v7x, 32 devices: a whole 2x2x4 slice. The times are simulated.
32 devices in a mesh: row: 4 (over x, core), col: 8 (over z, y).
Axes of the slice: x: 2, y: 2, z: 4, core: 2. Of those that a mesh axis runs over, the one named last changes fastest.
Arguments:
- tokens: bfloat16 [3584, 4096], P('col', 'row'), may hold values from -50 to 50
- ln_gain: float32 [4096], P('row'), may hold values from 0.1 to 1.9
- ln_shift: float32 [4096], P('row'), may hold values from -4 to 4
- w_qkv: bfloat16 [4096, 12288], P('row', 'col'), may hold values from -2 to 2
- w_out: bfloat16 [4096, 4096], P('col', 'row'), may hold values from -0.09375 to 0.09375
- layer_scale: float32 [4096], P('row'), may hold values from 0.5 to 2
- segments: int32 [3584], replicated, may hold values from 0 to 8, as said below
- present: int32 [3584], replicated, may hold values from 0 to 1, as said below
- coords: int32 [2, 3584], replicated, may hold values from 0 to 22, as said below
- owner_slot: int32 [3584], replicated, may hold values from 0 to 3583, as said below
Outputs:
- layer_out: bfloat16 [3584, 4096], P('col', 'row')
Inputs may be any that keep to these rules, and one draw needn't show every extreme that they name: `segments`: the picture of each token, pictures numbered in stream order; each picture's tokens form one run, pictures follow each other from position 0, and the padding tokens after them carry 8. `present`: 1 exactly where segments is below 8. A picture has h rows of w patches, 8 <= h <= 18 and 12 <= w <= 22, and some picture has 18 rows of 22; its first 5 tokens (class and registers) have 0 in both rows of coords, then its patches follow in row-major order with patch row and column counted from 1; padding tokens have 0 in both. `owner_slot`: A permutation of the 3584 tokens onto slots. Each block of 896 slots (slot // 896) holds 2 whole pictures, each on consecutive slots in stream order, followed by padding tokens.
All inputs are finite; a program needn't handle non-finite values.
Results may differ from a plain program's by a relative error of at most 0.017.
Values may be sent and summed in bfloat16 or wider, within the bound.
No kernel may reach another device: no remote copies, remote signals or barrier semaphores. Data moves between devices by JAX's collectives and lax.ppermute only.
A program may use at most 64 MiB of HBM per device.

v0:
```python
import jax
import jax.numpy as jnp
from jax import lax
from jax.sharding import PartitionSpec as P

D = 4096
HD = 128


def rotate(values, row_pos, col_pos):
    quarter = values.shape[-1] // 4
    frequency = 100.0 ** (-jnp.arange(quarter, dtype=jnp.float32) / quarter)
    angles = jnp.concatenate(
        [row_pos[:, None] * frequency[None, :], col_pos[:, None] * frequency[None, :]], axis=1
    )
    cosine = jnp.cos(angles)[:, None, :]
    sine_wave = jnp.sin(angles)[:, None, :]
    former = jnp.concatenate(
        [values[..., :quarter], values[..., 2 * quarter : 3 * quarter]], axis=-1
    )
    latter = jnp.concatenate(
        [values[..., quarter : 2 * quarter], values[..., 3 * quarter :]], axis=-1
    )
    new_former = former * cosine - latter * sine_wave
    new_latter = latter * cosine + former * sine_wave
    return jnp.concatenate(
        [
            new_former[..., :quarter],
            new_latter[..., :quarter],
            new_former[..., quarter:],
            new_latter[..., quarter:],
        ],
        axis=-1,
    )


def normalize(values, totals, squares, ln_gain, ln_shift):
    average = totals / D
    spread = squares / D - average * average
    scale_inv = lax.rsqrt(spread + 1e-06)
    return ((values - average[:, None]) * scale_inv[:, None] * ln_gain + ln_shift).astype(
        jnp.bfloat16
    )


def local(
    tokens, ln_gain, ln_shift, w_qkv, w_out, layer_scale, segments, present, coords, owner_slot
):
    own_rows = tokens.astype(jnp.float32)
    totals, squares = lax.psum(
        (jnp.sum(own_rows, axis=1), jnp.sum(own_rows * own_rows, axis=1)), "row"
    )
    normed = normalize(own_rows, totals, squares, ln_gain, ln_shift)
    gathered = lax.all_gather(normed, "col", axis=0, tiled=True)
    slot_count = owner_slot.shape[0]
    at_slot = (
        jnp.zeros((slot_count,), jnp.int32)
        .at[owner_slot]
        .set(jnp.arange(slot_count, dtype=jnp.int32))
    )
    placed = gathered[at_slot]
    group_rows = slot_count // lax.axis_size("row")
    mixed = lax.psum_scatter(
        jnp.dot(placed, w_qkv, preferred_element_type=jnp.float32).astype(jnp.bfloat16),
        "row",
        scatter_dimension=0,
        tiled=True,
    ).astype(jnp.float32)
    heads_here = w_qkv.shape[1] // (3 * HD)
    mixed = mixed.reshape(group_rows, heads_here, 3, HD)
    my_slots = lax.dynamic_slice_in_dim(at_slot, lax.axis_index("row") * group_rows, group_rows, 0)
    row_pos = coords[0][my_slots].astype(jnp.float32)
    col_pos = coords[1][my_slots].astype(jnp.float32)
    seg_rows = segments[my_slots]
    live_rows = present[my_slots]
    query_rows = rotate(mixed[:, :, 0], row_pos, col_pos).astype(jnp.bfloat16)
    key_rows = rotate(mixed[:, :, 1], row_pos, col_pos).astype(jnp.bfloat16)
    values = mixed[:, :, 2].astype(jnp.bfloat16)
    scores = jnp.einsum(
        "qhe,khe->hqk", query_rows, key_rows, preferred_element_type=jnp.float32
    ) * HD ** (-0.5)
    allowed = (seg_rows[:, None] == seg_rows[None, :]) & (live_rows[None, :] == 1)
    scores = jnp.where(allowed[None], scores, -1e30)
    highest = jnp.max(scores, axis=-1, keepdims=True)
    weights = jnp.exp(scores - highest)
    probability = (weights / jnp.sum(weights, axis=-1, keepdims=True)).astype(jnp.bfloat16)
    result = jnp.einsum("hqk,khe->qhe", probability, values, preferred_element_type=jnp.float32)
    attended = (result * live_rows[:, None, None].astype(jnp.float32)).astype(jnp.bfloat16)
    attended = attended.reshape(group_rows, heads_here * HD)
    all_slots = lax.all_gather(attended, "row", axis=0, tiled=True)
    projected = lax.psum_scatter(
        jnp.dot(all_slots[owner_slot], w_out, preferred_element_type=jnp.float32).astype(
            jnp.bfloat16
        ),
        "col",
        scatter_dimension=0,
        tiled=True,
    ).astype(jnp.float32)
    return (own_rows + layer_scale * projected).astype(jnp.bfloat16)


def solution(mesh):
    in_specs = (
        P("col", "row"),
        P("row"),
        P("row"),
        P("row", "col"),
        P("col", "row"),
        P("row"),
        P(),
        P(),
        P(),
        P(),
    )
    out_specs = P("col", "row")
    return jax.shard_map(local, mesh=mesh, in_specs=in_specs, out_specs=out_specs, check_vma=False)
```

profile of v0, /device:TPU:0, one launch (start us, length us, event | category | flops | bytes accessed | tf_op | source)
XLA Modules:
  0.0 506.5 jit_solution(16497828005602786089)
XLA Ops:
  6.5 0.0 copy-start
  6.5 0.0 copy-start.8
  6.5 0.0 all-gather.3.cloned.1.call-start
  6.5 1.7 convert_reduce_fusion
  8.2 8.3 %all-reduce = (f32[448]{0:T(512)S(1)}, f32[448]{0:T(512)S(1)}) all-reduce(f32[448]{0:T(512)S(1)} %get-tuple-element.6, f32[448]{0:T(512)S(1)} %get-tuple-element.5), channel_id=1, replica_groups=mesh['row'=4,'col'=8] {'row'}, use_global_device_ids=true, to_apply=%region_3.0 | all-reduce | flops 896 | bytes 7168 | tf_op jit(solution)/shard_map/psum | solution.py:50
  16.6 2.5 fusion.9
  19.1 0.0 all-gather.3.cloned.1.call-update
  19.1 0.0 reduce-scatter.3.cloned.1.call-start
  19.2 0.0 copy-done.8
  19.2 13.7 %scatter_custom_fusion = s32[3584]{0:T(1024)S(1)} fusion(s32[3584]{0:T(1024)S(1)} %compare_select_fusion.1, s32[3584]{0:T(1024)S(1)} %iota.11, s32[]{:T(128)} %constant.16.clone.1), kind=kCustom, calls=%fused_computation.56 | custom fusion | bytes 14340 | tf_op jit(solution)/shard_map/scatter | solution.py:59
  32.9 98.7 %all-gather.3.cloned.1.call-done = bf16[3584,1024]{1,0:T(8,128)(2,1)} async-done(((bf16[448,1024]{1,0:T(8,128)(2,1)}), bf16[3584,1024]{1,0:T(8,128)(2,1)}) %all-gather.3.cloned.1.call-update) | async-done | bytes 7340048 | tf_op jit(solution)/shard_map/all_gather | solution.py:54
  131.6 20.4 %gather_fusion = bf16[3584,1024]{1,0:T(8,128)(2,1)} fusion(bf16[3584,1024]{1,0:T(8,128)(2,1)} %all-gather.3.cloned.1.call-done, s32[4096]{0:T(1024)S(1)} %pad_clamp_fusion.1), kind=kCustom, calls=%fused_computation | custom fusion | bytes 14694400 | tf_op jit(solution)/shard_map/gather | solution.py:61
  152.0 0.0 copy-done
  152.0 16.9 %convolution_convert_fusion = bf16[3584,1536]{1,0:T(8,128)(2,1)} fusion(bf16[3584,1024]{1,0:T(8,128)(2,1)} %gather_fusion, bf16[1024,1536]{1,0:T(8,128)(2,1)S(1)} %copy-done), kind=kOutput, calls=%fused_computation.8 | convolution fusion | flops 11279794176 | bytes 21495808 | tf_op jit(solution)/shard_map/dot_general | solution.py:64
  169.0 0.0 reduce-scatter.3.cloned.1.call-update
  169.0 0.0 copy-start.2
  169.0 0.2 all-gather.5.cloned.1.call-start
  169.3 0.1 compare_select_fusion.2
  169.3 0.4 copy-done.2
  169.7 0.0 copy-start.3
  169.7 5.2 %gather_fusion.2 = s32[896]{0:T(1024)S(1)} fusion(s32[3584]{0:T(1024)S(1)} %copy-done.2, s32[1024]{0:T(1024)S(1)} %pad_clamp_fusion.2), kind=kCustom, calls=%fused_computation.2 | custom fusion | bytes 10752 | tf_op jit(solution)/shard_map/gather | solution.py:75
  174.9 0.0 copy-done.3
  174.9 0.0 copy-start.7
  174.9 5.2 %gather_fusion.1 = s32[896]{0:T(1024)S(1)} fusion(s32[3584]{0:T(1024)S(1)} %copy-done.3, s32[1024]{0:T(1024)S(1)} %pad_clamp_fusion.2), kind=kCustom, calls=%fused_computation.1 | custom fusion | bytes 10752 | tf_op jit(solution)/shard_map/gather | solution.py:74
  180.1 0.0 copy-done.7
  180.1 0.1 slice_reduce_fusion.1
  180.2 5.2 %gather_fusion.3 = s32[896]{0:T(1024)S(1)} fusion(s32[3584]{0:T(1024)S(1)} %get-tuple-element.7, s32[1024]{0:T(1024)S(1)} %pad_clamp_fusion.2), kind=kCustom, calls=%fused_computation.3 | custom fusion | bytes 10752 | tf_op jit(solution)/shard_map/gather | solution.py:72
  185.4 5.2 %gather_fusion.4 = s32[896]{0:T(1024)S(1)} fusion(s32[3584]{0:T(1024)S(1)} %get-tuple-element.8, s32[1024]{0:T(1024)S(1)} %pad_clamp_fusion.2), kind=kCustom, calls=%fused_computation.4 | custom fusion | bytes 10752 | tf_op jit(solution)/shard_map/gather | solution.py:73
  190.6 0.3 broadcast_multiply_fusion.1
  190.9 2.6 fusion.15
  193.5 1.6 compare_and_fusion
  195.0 61.1 %reduce-scatter.3.cloned.1.call-done = bf16[896,1536]{1,0:T(8,128)(2,1)} async-done(((bf16[3584,1536]{1,0:T(8,128)(2,1)}), bf16[896,1536]{1,0:T(8,128)(2,1)}) %reduce-scatter.3.cloned.1.call-update) | async-done | bytes 2752528 | tf_op jit(solution)/shard_map/reduce_scatter | solution.py:63
  256.1 3.3 copy.15
  259.4 0.0 copy-start.4
  259.4 3.1 copy.17
  262.6 0.0 copy-done.4
  262.6 2.3 reshape.134
  264.8 1.5 slice_bitcast_fusion
  266.4 11.6 %fusion.20 = (f32[896,4,32]{2,0,1:T(8,128)}, f32[896,4,32]{2,0,1:T(8,128)}, f32[896,4,32]{2,0,1:T(8,128)}, f32[896,4,32]{2,0,1:T(8,128)}, f32[896,4,32]{2,0,1:T(...) fusion(f32[896,4,128]{2,0,1:T(8,128)S(1)} %get-tuple-element.15, ...), kind=kLoop, calls=%fused_computation.65 | loop fusion | bytes 7340032 | tf_op jit(solution)/shard_map/slice | solution.py:19
  278.0 6.7 %subtract_convert_fusion = (bf16[896,4,64]{2,0,1:T(8,128)(2,1)S(1)}, bf16[896,4,64]{2,0,1:T(8,128)(2,1)S(1)}, bf16[896,4,64]{2,0,1:T(8,128)(2,1)S(1)}, bf16[896,4,64]{2,0,1:T(8,128)(2,1)S(1)}) fusion(f32[896,64]{1,0:T(8,128)} %get-tuple-element.36, f32[896,64]{1,0:T(8,128)} %get-tuple-element.35, f32[896,4,32]{2,0,1:T(8,128)} %get-tuple-element.18, ...), kind=kLoop, calls=%fused_computation.37 | loop fusion | flops 4587520 | bytes 5963776 | tf_op jit(solution)/shard_map/convert.8
  284.6 1.6 fusion.22
  286.2 1.6 fusion.23
  287.8 1.6 fusion.25
  289.3 0.0 copy-start.5
  289.3 0.0 copy-start.6
  289.3 1.6 fusion.24
  290.9 0.0 copy-done.5
  290.9 0.4 copy-done.6
  291.3 12.0 %fusion.26 = (f32[4,896]{1,0:T(4,128)S(1)}, f32[4,896,896]{1,2,0:T(8,128)}) fusion(pred[896,896]{0,1:T(8,128)(4,1)} %compare_and_fusion, bf16[896,4,32]{2,0,1:T(8,128)(2,1)} %get-tuple-element.28, bf16[896,4,32]{2,0,1:T(8,128)(2,1)S(1)} %copy-done.6, bf16[896,4,32]{2,0,1:T(8,128)(2,1)} %get-tuple-element.27, bf16[896,4,32]{2,0,1:T(8,128)(2,1)S(1)} %copy-done.5, ...), kind=kOutput, calls=%fused_computation.71 | convolution fusion | flops 842269568 | bytes 15497216 | tf_op jit(solution)/shard_map/sub | solution.py:85
  303.3 6.2 %multiply_convert_fusion = bf16[4,128,896]{2,1,0:T(8,128)(2,1)S(1)} fusion(f32[4,896,896]{1,2,0:T(8,128)} %get-tuple-element.42, f32[4,896]{1,0:T(4,128)S(1)} %get-tuple-element.41, bf16[896,4,3,128]{0,3,2,1:T(8,128)(2,1)} %bitcast.19, f32[896]{0:T(1024)S(1)} %convert_element_type.63), kind=kOutput, calls=%fused_computation.35 | convolution fusion | flops 829423616 | bytes 14697984 | tf_op jit(solution)/shard_map/hqk,khe->qhe/dot_general | solution.py:87
  309.6 1.3 copy.19
  310.9 0.0 all-gather.5.cloned.1.call-update
  310.9 0.0 reduce-scatter.5.cloned.1.call-start
  311.0 0.0 copy-start.10
  311.0 31.6 %all-gather.5.cloned.1.call-done = bf16[3584,512]{1,0:T(8,128)(2,1)} async-done(((bf16[896,512]{1,0:T(8,128)(2,1)}), bf16[3584,512]{1,0:T(8,128)(2,1)}) %all-gather.5.cloned.1.call-update) | async-done | bytes 3670032 | tf_op jit(solution)/shard_map/all_gather | solution.py:90
  342.6 13.7 %gather_fusion.5 = bf16[3584,512]{1,0:T(8,128)(2,1)} fusion(bf16[3584,512]{1,0:T(8,128)(2,1)} %all-gather.5.cloned.1.call-done, s32[4096]{0:T(1024)S(1)} %pad_clamp_fusion), kind=kCustom, calls=%fused_computation.5 | custom fusion | bytes 7354368 | tf_op jit(solution)/shard_map/gather | solution.py:92
  356.3 0.0 copy-done.10
  356.3 8.1 %convolution_convert_fusion.1 = bf16[3584,1024]{1,0:T(8,128)(2,1)} fusion(bf16[3584,512]{1,0:T(8,128)(2,1)} %gather_fusion.5, bf16[512,1024]{1,0:T(8,128)(2,1)S(1)} %copy-done.10), kind=kOutput, calls=%fused_computation.13 | convolution fusion | flops 3761766400 | bytes 12058624 | tf_op jit(solution)/shard_map/dot_general | solution.py:92
  364.4 0.0 reduce-scatter.5.cloned.1.call-update
  364.4 0.0 copy-start.1
  364.4 132.8 %reduce-scatter.5.cloned.1.call-done = bf16[448,1024]{1,0:T(8,128)(2,1)} async-done(((bf16[3584,1024]{1,0:T(8,128)(2,1)}), bf16[448,1024]{1,0:T(8,128)(2,1)}) %reduce-scatter.5.cloned.1.call-update) | async-done | bytes 917520 | tf_op jit(solution)/shard_map/reduce_scatter | solution.py:91
  497.2 0.0 copy-done.9
  497.2 2.7 fusion.11
  500.0 0.0 copy-done.1
  (13 shorter events, 0.1 us)
Async XLA Ops:
  6.5 145.5 %copy-start = (bf16[1024,1536]{1,0:T(8,128)(2,1)S(1)}, bf16[1024,1536]{1,0:T(8,128)(2,1)}, u32[]{:S(2)}) copy-start(bf16[1024,1536]{1,0:T(8,128)(2,1)} %param.13) | copy-start | bytes 9437188
  6.5 12.7 %copy-start.8 = (s32[3584]{0:T(1024)S(1)}, s32[3584]{0:T(1024)}, u32[]{:S(2)}) copy-start(s32[3584]{0:T(1024)} %param.19) | copy-start | bytes 43012
  6.5 125.1 %all-gather.3.cloned.1.call-start = ((), (), s32[]{:S(2)}) async-start(), calls=%async_computation.2 | async-start | bytes 8257536 | tf_op jit(solution)/shard_map/all_gather | solution.py:54
  19.1 237.0 %reduce-scatter.3.cloned.1.call-start = ((), (), s32[]{:S(2)}) async-start(), calls=%async_computation.3 | async-start | bytes 13762560 | tf_op jit(solution)/shard_map/reduce_scatter | solution.py:63
  169.0 0.7 copy-start.2
  169.0 173.5 %all-gather.5.cloned.1.call-start = ((), (), s32[]{:S(2)}) async-start(), calls=%async_computation.4 | async-start | bytes 4587520 | tf_op jit(solution)/shard_map/all_gather | solution.py:90
  169.7 5.2 %copy-start.3 = (s32[3584]{0:T(1024)S(1)}, s32[3584]{0:T(1024)}, u32[]{:S(2)}) copy-start(s32[3584]{0:T(1024)} %param.16) | copy-start | bytes 43012
  174.9 5.2 %copy-start.7 = (s32[2,3584]{1,0:T(2,128)S(1)}, s32[2,3584]{1,0:T(2,128)}, u32[]{:S(2)}) copy-start(s32[2,3584]{1,0:T(2,128)} %param.18) | copy-start | bytes 86020
  259.4 3.1 copy-start.4
  289.3 1.6 copy-start.5
  289.3 2.0 copy-start.6
  310.9 186.3 %reduce-scatter.5.cloned.1.call-start = ((), (), s32[]{:S(2)}) async-start(), calls=%async_computation.5 | async-start | bytes 8257536 | tf_op jit(solution)/shard_map/reduce_scatter | solution.py:91
  311.0 45.3 %copy-start.10 = (bf16[512,1024]{1,0:T(8,128)(2,1)S(1)}, bf16[512,1024]{1,0:T(8,128)(2,1)}, u32[]{:S(2)}) copy-start(bf16[512,1024]{1,0:T(8,128)(2,1)} %param.14) | copy-start | bytes 3145732
  364.4 132.8 %copy-start.9 = (f32[1024]{0:T(1024)S(1)}, f32[1024]{0:T(1024)}, u32[]{:S(2)}) copy-start(f32[1024]{0:T(1024)} %param.15) | copy-start | bytes 12292
  364.4 135.5 %copy-start.1 = (bf16[1024,1536]{1,0:T(8,128)(2,1)S(1)}, bf16[1024,1536]{1,0:T(8,128)(2,1)}, u32[]{:S(2)}) copy-start(bf16[1024,1536]{1,0:T(8,128)(2,1)} %param.13) | copy-start | bytes 9437188
Sparse Core Ops, SparseCore 0:
  19.3 112.3 all-gather.2
  169.1 86.9 reduce-scatter.2
  311.0 31.5 all-gather.4
  364.5 132.6 reduce-scatter.4
where the time goes:
time: 507 us; the launch traced here: 506 us
  waiting for transfers between devices  324 us (64%)
  local copies, waits for them, and re-layouts  96.5 us (19%)
  matrix products  43.3 us (9%)
  other arithmetic  20.5 us (4%)
  between operations  13.4 us (3%)
  blocking collectives  8.34 us (2%)
    reduce_scatter x1, waiting for transfers between devices, local(): lax.psum_scatter(jnp.dot(all_slots[owner_slot], w_out, preferred_element_...  133 us
    all_gather x1, waiting for transfers between devices, local(): gathered = lax.all_gather(normed, 'col', axis=0, tiled=True)  98.7 us
    reduce_scatter x1, waiting for transfers between devices, local(): lax.psum_scatter(jnp.dot(placed, w_qkv, preferred_element_type=jnp.float3...  61.1 us
    all_gather x1, waiting for transfers between devices, local(): all_slots = lax.all_gather(attended, 'row', axis=0, tiled=True)  31.6 us
    gather x1, local copies, waits for them, and re-layouts, local(): placed = gathered[at_slot]  20.4 us
    dot_general x1, matrix products, local(): jnp.dot(placed, w_qkv, preferred_element_type=jnp.float32)  16.9 us
    gather x1, local copies, waits for them, and re-layouts, local(): all_slots[owner_slot]  13.7 us
    scatter x1, local copies, waits for them, and re-layouts, local(): at_slot = jnp.zeros((slot_count,), jnp.int32).at[owner_slot].set(jnp.aran...  13.7 us
  transfers between devices with their start and end apart: 4, of which 4 were waited for; matrix products, arithmetic and copies ran while one was open for 8% of the time, Pallas kernels for 0%

commit v1 on v0

--- a/solution.py
+++ b/solution.py
@@ -1,10 +1,19 @@
+import functools
+
 import jax
 import jax.numpy as jnp
 from jax import lax
+from jax.experimental import pallas as pl
+from jax.experimental.pallas import tpu as pltpu
 from jax.sharding import PartitionSpec as P
 
 D = 4096
 HD = 128
+BF = jnp.bfloat16
+F32 = jnp.float32
+LONGEST = 5 + 18 * 22
+POSITIONS = 32
+MIB = 1024 * 1024
 
 
 def rotate(values, row_pos, col_pos):
@@ -43,7 +52,7 @@
     )
 
 
-def local(
+def local_general(
     tokens, ln_gain, ln_shift, w_qkv, w_out, layer_scale, segments, present, coords, owner_slot
 ):
     own_rows = tokens.astype(jnp.float32)
@@ -99,6 +108,321 @@
     return (own_rows + layer_scale * projected).astype(jnp.bfloat16)
 
 
+def whole(memory_space=pltpu.VMEM):
+    return pl.BlockSpec(memory_space=memory_space)
+
+
+def qkv_kernel(own, peer, stats, affine_own, affine_peer, w_own, w_peer, keep, send, normed):
+    columns = jnp.transpose(stats[...])
+    average, scale_inv = columns[:, 0:1], columns[:, 1:2]
+    width = own.shape[1]
+    for part, (rows, affine) in enumerate(((own, affine_own), (peer, affine_peer))):
+        for start in range(0, width, 256):
+            piece = slice(start, start + 256)
+            out = (rows[:, piece].astype(F32) - average) * scale_inv
+            out = out * affine[0:1, piece] + affine[1:2, piece]
+            normed[:, part * width + start : part * width + start + 256] = out.astype(BF)
+    half = keep.shape[1]
+    for target, first in ((send, half), (keep, 0)):
+        total = jnp.dot(
+            normed[:, :width], w_own[:, first : first + half], preferred_element_type=F32
+        )
+        total += jnp.dot(
+            normed[:, width:], w_peer[:, first : first + half], preferred_element_type=F32
+        )
+        target[...] = total.astype(BF)
+
+
+def qkv_block(own, peer, stats, affine_own, affine_peer, w_own, w_peer):
+    rows, width = own.shape
+    half = w_own.shape[1] // 2
+    out = jax.ShapeDtypeStruct((rows, half), BF)
+    return pl.pallas_call(
+        qkv_kernel,
+        out_shape=(out, out),
+        in_specs=[whole()] * 7,
+        out_specs=(whole(), whole()),
+        scratch_shapes=[pltpu.VMEM((rows, 2 * width), BF)],
+        compiler_params=pltpu.CompilerParams(vmem_limit_bytes=32 * MIB),
+        cost_estimate=pl.CostEstimate(
+            flops=2 * rows * 2 * width * 2 * half,
+            bytes_accessed=4 * rows * width + 8 * width * half + 4 * rows * half,
+            transcendentals=0,
+        ),
+        name="qkv_block",
+    )(own, peer, stats, affine_own, affine_peer, w_own, w_peer)
+
+
+def attend_kernel(tile, window, blocks, places, lows, seg_col, seg_row, table, *refs):
+    pairs, (out, query, key, value) = refs[: 2 * blocks], refs[2 * blocks :]
+    rows = pairs[0].shape[0]
+    lane = lax.broadcasted_iota(jnp.int32, (rows, HD), 1)
+    first_half = (lane % 64) < 32
+
+    for m in range(blocks):
+        at = pl.ds(pl.multiple_of(places[m] * rows, 16), rows)
+        cosine = table[at, :HD]
+        sine = table[at, HD:]
+
+        def turned(part):
+            cols = slice(part * HD, (part + 1) * HD)
+            both = pairs[m][:, cols].astype(F32) + pairs[blocks + m][:, cols].astype(F32)
+            if part == 2:
+                return both.astype(BF)
+            swapped = jnp.where(
+                first_half, pltpu.roll(both, HD - 32, 1), pltpu.roll(both, 32, 1)
+            )
+            return (both * cosine + swapped * sine).astype(BF)
+
+        query[at, :] = turned(0)
+        key[at, :] = turned(1)
+        value[at, :] = turned(2)
+
+    scale = HD ** (-0.5) * 1.4426950408889634
+
+    def step(i, carry):
+        at = pl.ds(pl.multiple_of(i * tile, tile), tile)
+        near = pl.ds(pl.multiple_of(lows[i], 128), window)
+        scores = (
+            lax.dot_general(
+                query[at, :],
+                key[near, :],
+                (((1,), (1,)), ((), ())),
+                preferred_element_type=F32,
+            )
+            * scale
+        )
+        marks = seg_col[at, :]
+        scores = jnp.where(marks == seg_row[0:1, near], scores, -1e30)
+        highest = jnp.max(scores, axis=1, keepdims=True)
+        weights = jnp.exp2(scores - highest)
+        total = jnp.sum(weights, axis=1, keepdims=True)
+        result = jnp.dot(weights.astype(BF), value[near, :], preferred_element_type=F32)
+        live = jnp.where(marks >= 0, 1.0 / total, 0.0)
+        out[at, :] = (result * live).astype(BF)
+        return carry
+
+    lax.fori_loop(0, out.shape[0] // tile, step, 0)
+
+
+def attend(places, lows, seg_col, seg_row, table, kept, received, tile, window):
+    blocks = len(kept)
+    count = seg_col.shape[0]
+    smem = whole(pltpu.SMEM)
+    return pl.pallas_call(
+        functools.partial(attend_kernel, tile, window, blocks),
+        out_shape=jax.ShapeDtypeStruct((count, HD), BF),
+        in_specs=[smem, smem] + [whole()] * (3 + 2 * blocks),
+        out_specs=whole(),
+        scratch_shapes=[pltpu.VMEM((count, HD), BF)] * 3,
+        compiler_params=pltpu.CompilerParams(vmem_limit_bytes=48 * MIB),
+        cost_estimate=pl.CostEstimate(
+            flops=4 * count * window * HD,
+            bytes_accessed=count * HD * 26,
+            transcendentals=count * window,
+        ),
+        name="attend",
+    )(places, lows, seg_col, seg_row, table, *kept, *received)
+
+
+def project_kernel(blocks, where, tokens, layer_scale, *refs):
+    weights = refs[:blocks]
+    parts = refs[blocks : 5 * blocks]
+    out, total = refs[5 * blocks :]
+    even = where[0] == 0
+    for m in range(blocks):
+        for pair in range(2):
+            one = parts[(2 * pair) * blocks + m][...]
+            two = parts[(2 * pair + 1) * blocks + m][...]
+            rows = jnp.concatenate(
+                [jnp.where(even, one, two), jnp.where(even, two, one)], axis=1
+            )
+            start = pl.multiple_of(where[1 + pair], 2 * HD)
+            term = jnp.dot(
+                rows, weights[m][pl.ds(start, 2 * HD), :], preferred_element_type=F32
+            )
+            if m == 0 and pair == 0:
+                total[...] = term
+            else:
+                total[...] += term
+    out[...] = (tokens[...].astype(F32) + layer_scale[...] * total[...]).astype(BF)
+
+
+def project(where, tokens, layer_scale, weights, parts):
+    blocks = len(weights)
+    return pl.pallas_call(
+        functools.partial(project_kernel, blocks),
+        out_shape=jax.ShapeDtypeStruct(tokens.shape, BF),
+        in_specs=[whole(pltpu.SMEM)] + [whole()] * (2 + 5 * blocks),
+        out_specs=whole(),
+        scratch_shapes=[pltpu.VMEM(tokens.shape, F32)],
+        compiler_params=pltpu.CompilerParams(vmem_limit_bytes=48 * MIB),
+        name="project",
+    )(where, tokens, layer_scale, *weights, *parts)
+
+
+def local_heads(
+    tokens, ln_gain, ln_shift, w_qkv, w_out, layer_scale, segments, present, coords, owner_slot
+):
+    rows = lax.axis_size("row")
+    cols = lax.axis_size("col")
+    count = segments.shape[0]
+    block = tokens.shape[0]
+    row = lax.axis_index("row")
+    col = lax.axis_index("col")
+    core, x_index = row % 2, row // 2
+    head = 2 * core + x_index
+
+    lines = cols // 2
+    ring = list(range(0, lines, 2)) + list(range(lines - 1 - lines % 2, 0, -2))
+    after = {z: ring[(i + 1) % lines] for i, z in enumerate(ring)}
+    y_swap = [(c, c ^ 1) for c in range(cols)]
+    z_next = [(2 * z + y, 2 * after[z] + y) for z in range(lines) for y in range(2)]
+    core_swap = [(r, r ^ 1) for r in range(rows)]
+    x_swap = [(r, r ^ 2) for r in range(rows)]
+
+    def by_y(value):
+        return lax.ppermute(value, "col", y_swap)
+
+    def by_z(value):
+        return lax.ppermute(value, "col", z_next)
+
+    def by_core(value):
+        return lax.ppermute(value, "row", core_swap)
+
+    def by_x(value):
+        return lax.ppermute(value, "row", x_swap)
+
+    def hold(*values):
+        return lax.optimization_barrier(values)
+
+    source = {}
+    for c in range(cols):
+        z, y = c // 2, c % 2
+        back = {b: a for a, b in after.items()}
+        for i in range(lines):
+            source[c, i] = 2 * z + y
+            source[c, lines + i] = 2 * z + 1 - y
+            z = back[z]
+    places = jnp.asarray([[source[c, m] for m in range(cols)] for c in range(cols)], jnp.int32)[col]
+    targets = [{source[c, m]: c for c in range(cols)} for m in range(cols)]
+    send_to = jnp.asarray([[targets[m][c] for m in range(cols)] for c in range(cols)], jnp.int32)[
+        col
+    ]
+
+    own_rows = tokens.astype(F32)
+    sums = lax.psum(
+        jnp.stack([jnp.sum(own_rows, axis=1), jnp.sum(own_rows * own_rows, axis=1)]), "row"
+    )
+    average = sums[0] / D
+    spread = sums[1] / D - average * average
+    own_stats = jnp.concatenate(
+        [average[None], lax.rsqrt(spread + 1e-06)[None], jnp.zeros((6, block), F32)]
+    )
+
+    width = 3 * HD
+
+    def head_columns(which):
+        return lax.dynamic_slice_in_dim(w_qkv, which * width, width, 1)
+
+    w_own = jnp.concatenate([head_columns(head), head_columns(head ^ 1)], axis=1)
+    w_peer = by_core(jnp.concatenate([head_columns(head ^ 2), head_columns(head ^ 3)], axis=1))
+    affine_own = jnp.stack([ln_gain, ln_shift])
+    affine_peer = by_core(affine_own)
+
+    def qkv(own, peer, stats):
+        return qkv_block(own, peer, stats, affine_own, affine_peer, w_own, w_peer)
+
+    z_tok, z_stat = [tokens], [own_stats]
+    y_tok, y_stat = [], []
+    for i in range(lines):
+        y_new, y_s = by_y(z_tok[i]), by_y(z_stat[i])
+        if i < lines - 1:
+            z_new, z_s = by_z(z_tok[i]), by_z(z_stat[i])
+            z_new, y_new, z_s, y_s = hold(z_new, y_new, z_s, y_s)
+            z_tok.append(z_new)
+            z_stat.append(z_s)
+        y_tok.append(y_new)
+        y_stat.append(y_s)
+    blocks_tok, blocks_stat = z_tok + y_tok, z_stat + y_stat
+    kept, received = [], []
+    for own, stats in zip(blocks_tok, blocks_stat):
+        keep, send = qkv(own, by_core(own), stats)
+        kept.append(keep)
+        received.append(by_x(send))
+
+    w_first, _ = hold(w_out, z_tok[-1])
+    z_w, y_w = [w_first], []
+    for i in range(lines):
+        y_new = by_y(z_w[i])
+        if i < lines - 1:
+            z_new = by_z(z_w[i])
+            z_new, y_new = hold(z_new, y_new)
+            z_w.append(z_new)
+        y_w.append(y_new)
+    weights = z_w + y_w
+
+    quarter = HD // 4
+    frequency = 100.0 ** (-jnp.arange(quarter, dtype=F32) / quarter)
+    angles = jnp.arange(POSITIONS, dtype=F32)[:, None] * frequency[None, :]
+    cosine, sine = jnp.cos(angles), jnp.sin(angles)
+    none = jnp.zeros((POSITIONS, 2 * quarter), F32)
+    cos_pair = jnp.concatenate([cosine, cosine], axis=1)
+    sin_pair = jnp.concatenate([-sine, sine], axis=1)
+    turns = jnp.concatenate(
+        [
+            jnp.concatenate([cos_pair, none, sin_pair, none], axis=1),
+            jnp.concatenate([none, cos_pair, none, sin_pair], axis=1),
+        ],
+        axis=0,
+    )
+    spots = jnp.arange(POSITIONS, dtype=jnp.int32)
+    chosen = jnp.concatenate(
+        [coords[0][:, None] == spots[None, :], coords[1][:, None] == spots[None, :]], axis=1
+    )
+    table = jnp.dot(
+        chosen.astype(F32),
+        turns,
+        precision=lax.Precision.HIGHEST,
+        preferred_element_type=F32,
+    )
+
+    tile = 256
+    reach = -(-(LONGEST - 1) // 128) * 128
+    window = min(count, tile + 2 * reach)
+    tiles = count // tile
+    marks = jnp.where(present == 1, segments, -1)
+    lows = jnp.clip(jnp.arange(tiles, dtype=jnp.int32) * tile - reach, 0, count - window)
+    attended = attend(
+        places,
+        lows,
+        marks[:, None],
+        marks[None, :],
+        table,
+        kept,
+        received,
+        tile,
+        window,
+    )
+
+    parts = []
+    for m in range(cols):
+        piece = lax.dynamic_slice_in_dim(attended, send_to[m] * block, block, 0)
+        pairs = [(c, targets[m][c]) for c in range(cols)]
+        parts.append(piece if m == 0 else lax.ppermute(piece, "col", pairs))
+    x_parts = [by_x(piece) for piece in parts]
+    c_parts = [by_core(piece) for piece in parts]
+    d_parts = [by_core(piece) for piece in x_parts]
+    where = jnp.stack([x_index, core * 2 * HD, (1 - core) * 2 * HD]).astype(jnp.int32)
+    return project(
+        where,
+        tokens,
+        layer_scale[None, :],
+        weights,
+        parts + x_parts + c_parts + d_parts,
+    )
+
+
 def solution(mesh):
     in_specs = (
         P("col", "row"),
@@ -113,4 +437,12 @@
         P(),
     )
     out_specs = P("col", "row")
+    rows, cols = mesh.shape["row"], mesh.shape["col"]
+
+    def local(*args):
+        heads_here = args[3].shape[1] // (3 * HD)
+        if rows == 4 and heads_here == 4 and cols % 2 == 0 and args[6].shape[0] % 256 == 0:
+            return local_heads(*args)
+        return local_general(*args)
+
     return jax.shard_map(local, mesh=mesh, in_specs=in_specs, out_specs=out_specs, check_vma=False)

time: 507 us -> 304 us (0.60)
  waiting for transfers between devices: 324 us -> 113 us
  starting transfers between devices: 0.31 us -> 66 us
  Pallas kernels: 0 us -> 53.2 us
  local copies, waits for them, and re-layouts: 96.5 us -> 48.2 us
  matrix products: 43.3 us -> 4.56 us
  other arithmetic: 20.5 us -> 4.86 us
  between operations: 13.4 us -> 5.63 us
    reduce_scatter x2 -> x0, waiting for transfers between devices: 194 us -> none  [the longest x1 133 us: local(): lax.psum_scatter(jnp.dot(all_slots[owner_slot], w_out, preferred_element_...]
    all_gather x2 -> x0, waiting for transfers between devices: 130 us -> none  [the longest x1 98.7 us: local(): gathered = lax.all_gather(normed, 'col', axis=0, tiled=True)]
    ppermute x0 -> x70, waiting for transfers between devices: none -> 113 us  [the longest x9 49 us: by_z(): return lax.ppermute(value, 'col', z_next)]
    ppermute x0 -> x70, starting transfers between devices: none -> 66 us  [the longest x16 20.8 us: by_x(): return lax.ppermute(value, 'row', x_swap)]
    gather x6 -> x0, local copies, waits for them, and re-layouts: 54.8 us -> none  [the longest x1 20.4 us: local(): placed = gathered[at_slot]]
    pallas_call x0 -> x10, Pallas kernels: none -> 53.2 us  [the longest x8 26.4 us: qkv_block(): pl.pallas_call(qkv_kernel, out_shape=(out, out), in_specs=[whole()] * 7,...]
    unnamed x22 -> x168, local copies, waits for them, and re-layouts: 0.84 us -> 37.1 us
    dot_general x3 -> x1, matrix products: 31.3 us -> 4.56 us  [local_heads(): jnp.dot(chosen.astype(F32), turns, precision=lax.Precision.HIGHEST, prefe...]
  transfers between devices with their start and end apart: 4 -> 70, of which waited for: 4 -> 27; matrix products, arithmetic and copies ran while one was open for 8% -> 7% of each run, Pallas kernels for 0% -> 15%
where the time goes in v1:
time: 304 us; the launch traced here: 302 us
  waiting for transfers between devices  113 us (37%)
  starting transfers between devices  66 us (22%)
  Pallas kernels  53.2 us (18%)
  local copies, waits for them, and re-layouts  48.2 us (16%)
  blocking collectives  6.43 us (2%)
  between operations  5.63 us (2%)
  other arithmetic  4.86 us (2%)
  matrix products  4.56 us (1%)
    ppermute x9, waiting for transfers between devices, by_z(): return lax.ppermute(value, 'col', z_next)  49 us
    unnamed x168, local copies, waits for them, and re-layouts  37.1 us
    pallas_call x8, Pallas kernels, qkv_block(): pl.pallas_call(qkv_kernel, out_shape=(out, out), in_specs=[whole()] * 7,...  26.4 us
    ppermute x12, waiting for transfers between devices, by_y(): return lax.ppermute(value, 'col', y_swap)  23.5 us
    ppermute x16, starting transfers between devices, by_x(): return lax.ppermute(value, 'row', x_swap)  20.8 us
    ppermute x7, waiting for transfers between devices, local_heads(): parts.append(piece if m == 0 else lax.ppermute(piece, 'col', pairs))  19.5 us
    ppermute x16, waiting for transfers between devices, by_x(): return lax.ppermute(value, 'row', x_swap)  19.1 us
    pallas_call x1, Pallas kernels, attend(): pl.pallas_call(functools.partial(attend_kernel, tile, window, blocks), ou...  18.6 us
  transfers between devices with their start and end apart: 70, of which 27 were waited for; matrix products, arithmetic and copies ran while one was open for 7% of the time, Pallas kernels for 15%

profile of v1, /device:TPU:0, one launch (start us, length us, event | category | flops | bytes accessed | tf_op | source)
XLA Modules:
  0.0 302.3 jit_solution(14841574989213517199)
XLA Ops:
  0.0 4.0 %collective-permute-start = (bf16[448,1024]{1,0:T(8,128)(2,1)}, bf16[448,1024]{1,0:T(8,128)(2,1)}, u32[]{:S(2)}, u32[]{:S(2)}) collective-permute-start(bf16[448,1024]{1,0:T(8,128)(2,1)} %tokens.1), channel_id=1, source_target_pairs={{0,4},{1,5},{2,0},{3,1},{4,6},{5,7},{6,2},{7,3},{8,12},{9,13},{10,... | collective-permute-start | bytes 2752520 | tf_op jit(solution)/shard_map/ppermute | solution.py:288
  4.0 1.5 collective-permute-start.1
  5.6 1.5 convert_reduce_fusion
  7.2 6.4 %psum.7 = f32[2,448]{1,0:T(2,128)S(1)} all-reduce(f32[2,448]{1,0:T(2,128)S(1)} %pad_maximum_fusion.3), channel_id=1, replica_groups=mesh['row'=4,'col'=8] {'row'}, use_global_device_ids=true, to_apply=%region_2.3 | all-reduce | flops 896 | bytes 7168 | tf_op jit(solution)/shard_map/psum | solution.py:314
  13.7 1.6 collective-permute-start.2
  15.8 8.4 %collective-permute-done.2.stats = f32[8,448]{1,0:T(8,128)S(1)} collective-permute-done((f32[8,448]{1,0:T(8,128)S(1)}, f32[8,448]{1,0:T(8,128)S(1)}, u32[]{:S(2)}, u32[]{:S(2)}) %collective-permute-start.2) | collective-permute-done | bytes 14368 | tf_op jit(solution)/shard_map/ppermute | solution.py:288
  24.2 2.2 collective-permute-done.3.stats
  26.4 1.6 collective-permute-start.4
  28.1 1.5 collective-permute-start.5
  30.4 17.6 %collective-permute-done.6.stats = f32[8,448]{1,0:T(8,128)S(1)} collective-permute-done((f32[8,448]{1,0:T(8,128)S(1)}, f32[8,448]{1,0:T(8,128)S(1)}, u32[]{:S(2)}, u32[]{:S(2)}) %collective-permute-start.6) | collective-permute-done | bytes 14368 | tf_op jit(solution)/shard_map/ppermute | solution.py:288
  48.0 1.3 collective-permute-done.7.stats
  51.1 1.5 collective-permute-start.9
  52.6 2.2 constant_dynamic-slice_fusion.10
  55.8 14.6 %collective-permute-done.10.stats = f32[8,448]{1,0:T(8,128)S(1)} collective-permute-done((f32[8,448]{1,0:T(8,128)S(1)}, f32[8,448]{1,0:T(8,128)S(1)}, u32[]{:S(2)}, u32[]{:S(2)}) %collective-permute-start.10) | collective-permute-done | bytes 14368 | tf_op jit(solution)/shard_map/ppermute | solution.py:288
  70.4 1.5 collective-permute-start.11
  72.5 1.6 collective-permute-done.11.stats
  74.8 2.6 collective-permute-start.12
  77.4 1.5 collective-permute-start.13
  82.8 2.3 qkv_block.8
  86.4 1.5 collective-permute-start.31
  87.9 8.4 %collective-permute-done.12.refs_1_ = bf16[512,1024]{1,0:T(8,128)(2,1)} collective-permute-done((bf16[512,1024]{1,0:T(8,128)(2,1)S(1)}, bf16[512,1024]{1,0:T(8,128)(2,1)}, u32[]{:S(2)}, u32[]{:S(2)}) %collective-permute-start.12) | collective-permute-done | bytes 1048608 | tf_op jit(solution)/shard_map/ppermute | solution.py:288
  96.3 2.0 collective-permute-done.13.refs_4_
  99.2 1.5 collective-permute-start.28
  101.7 1.8 collective-permute-start.14
  104.9 1.3 compare_select_fusion
  106.8 15.9 %collective-permute-done.28.own = bf16[448,1024]{1,0:T(8,128)(2,1)} collective-permute-done((bf16[448,1024]{1,0:T(8,128)(2,1)}, bf16[448,1024]{1,0:T(8,128)(2,1)}, u32[]{:S(2)}, u32[]{:S(2)}) %collective-permute-start.28) | collective-permute-done | bytes 917536 | tf_op jit(solution)/shard_map/ppermute | solution.py:285
  125.5 1.4 copy-done.52
  129.5 3.7 %qkv_block.9 = (bf16[448,384]{1,0:T(8,128)(2,1)S(1)}, bf16[448,384]{1,0:T(8,128)(2,1)S(1)}) custom-call(bf16[448,1024]{1,0:T(8,128)(2,1)} %collective-permute-done.own, bf16[448,1024]{1,0:T(8,128)(2,1)S(1)} %copy-done.61, f32[8,448]{1,0:T(8,128)S(1)} %copy-done.65, f32[2,1024]{1,0:T(2,128)S(1)} %copy-done.49, f32[2,1024]{1,0:T(2,128)S(1)} %copy-done.75, ...), custom_call_target="tpu_custom_call" | custom-call | flops 1409286144 | bytes 5668864 | tf_op jit(solution)/shard_map/qkv_block/pallas_call | solution.py:140
  133.9 1.5 collective-permute-start.32
  135.4 3.5 %qkv_block.12 = (bf16[448,384]{1,0:T(8,128)(2,1)S(1)}, bf16[448,384]{1,0:T(8,128)(2,1)S(1)}) custom-call(bf16[448,1024]{1,0:T(8,128)(2,1)} %collective-permute-done.1.own, bf16[448,1024]{1,0:T(8,128)(2,1)S(1)} %copy-done.59, f32[8,448]{1,0:T(8,128)S(1)} %copy-done.63, f32[2,1024]{1,0:T(2,128)S(1)} %copy-done.49, f32[2,1024]{1,0:T(2,128)S(1)} %copy-done.75, ...), custom_call_target="tpu_custom_call" | custom-call | flops 1409286144 | bytes 5668864 | tf_op jit(solution)/shard_map/qkv_block/pallas_call | solution.py:140
  139.7 3.8 %qkv_block.10 = (bf16[448,384]{1,0:T(8,128)(2,1)S(1)}, bf16[448,384]{1,0:T(8,128)(2,1)S(1)}) custom-call(bf16[448,1024]{1,0:T(8,128)(2,1)} %collective-permute-done.4.own, bf16[448,1024]{1,0:T(8,128)(2,1)} %collective-permute-done.23.peer, f32[8,448]{1,0:T(8,128)S(1)} %copy-done.69, f32[2,1024]{1,0:T(2,128)S(1)} %copy-done.49, f32[2,1024]{1,0:T(2,128)S(1)} %copy-done.75, ...), custom_call_target="tpu_custom_call" | custom-call | flops 1409286144 | bytes 5668864 | tf_op jit(solution)/shard_map/qkv_block/pallas_call | solution.py:140
  145.6 1.5 collective-permute-start.30
  147.1 3.8 %qkv_block.13 = (bf16[448,384]{1,0:T(8,128)(2,1)S(1)}, bf16[448,384]{1,0:T(8,128)(2,1)S(1)}) custom-call(bf16[448,1024]{1,0:T(8,128)(2,1)} %collective-permute-done.5.own, bf16[448,1024]{1,0:T(8,128)(2,1)} %collective-permute-done.26.peer, f32[8,448]{1,0:T(8,128)S(1)} %copy-done.67, f32[2,1024]{1,0:T(2,128)S(1)} %copy-done.49, f32[2,1024]{1,0:T(2,128)S(1)} %copy-done.75, ...), custom_call_target="tpu_custom_call" | custom-call | flops 1409286144 | bytes 5668864 | tf_op jit(solution)/shard_map/qkv_block/pallas_call | solution.py:140
  151.7 1.5 collective-permute-start.35
  153.7 1.5 collective-permute-start.36
  155.2 1.4 collective-permute-start.16
  157.2 3.5 %qkv_block.11 = (bf16[448,384]{1,0:T(8,128)(2,1)S(1)}, bf16[448,384]{1,0:T(8,128)(2,1)}) custom-call(bf16[448,1024]{1,0:T(8,128)(2,1)} %collective-permute-done.8.own, bf16[448,1024]{1,0:T(8,128)(2,1)S(1)} %collective-permute-done.24.peer, f32[8,448]{1,0:T(8,128)S(1)} %copy-done.71, f32[2,1024]{1,0:T(2,128)S(1)} %copy-done.49, f32[2,1024]{1,0:T(2,128)S(1)} %copy-done.76, ...), custom_call_target="tpu_custom_call" | custom-call | flops 1409286144 | bytes 5668864 | tf_op jit(solution)/shard_map/qkv_block/pallas_call | solution.py:140
  161.4 2.3 qkv_block.14
  164.5 3.5 %qkv_block.15 = (bf16[448,384]{1,0:T(8,128)(2,1)S(1)}, bf16[448,384]{1,0:T(8,128)(2,1)}) custom-call(bf16[448,1024]{1,0:T(8,128)(2,1)} %collective-permute-done.28.own, bf16[448,1024]{1,0:T(8,128)(2,1)S(1)} %collective-permute-done.29.peer, f32[8,448]{1,0:T(8,128)S(1)} %collective-permute-done.30.stats, f32[2,1024]{1,0:T(2,128)S(1)} %copy-done.49, ...), custom_call_target="tpu_custom_call" | custom-call | flops 1409286144 | bytes 5668864 | tf_op jit(solution)/shard_map/qkv_block/pallas_call | solution.py:140
  170.8 1.5 collective-permute-start.34
  172.3 5.1 %collective-permute-done.36.refs_13_ = bf16[448,384]{1,0:T(8,128)(2,1)S(1)} collective-permute-done((bf16[448,384]{1,0:T(8,128)(2,1)S(1)}, bf16[448,384]{1,0:T(8,128)(2,1)S(1)}, u32[]{:S(2)}, u32[]{:S(2)}) %collective-permute-start.36) | collective-permute-done | bytes 344096 | tf_op jit(solution)/shard_map/ppermute | solution.py:294
  178.1 1.5 collective-permute-start.38
  180.5 1.5 concatenate.28
  182.0 3.0 broadcast_in_dim.31.seg_col
  190.8 4.6 %fusion.1.table = f32[3584,256]{1,0:T(8,128)} fusion(pred[3584,32]{0,1:T(32,128)(4,1)S(1)} %copy-done.79, pred[3584,32]{0,1:T(32,128)(4,1)} %get-tuple-element.105, f32[32,256]{1,0:T(8,128)} %concatenate.28, f32[32,256]{1,0:T(8,128)S(1)} %concatenate.27), kind=kOutput, calls=%fused_computation.5 | convolution fusion | flops 704888832 | bytes 3964928 | tf_op jit(solution)/shard_map/dot_general | solution.py:383
  195.4 2.6 collective-permute-done.38.refs_15_
  198.1 18.6 %attend.1 = bf16[3584,128]{1,0:T(8,128)(2,1)} custom-call(s32[8]{0:T(128)S(1)} %fusion.12.places, s32[14]{0:T(128)S(1)} %add_clamp_fusion.lows, s32[3584,1]{1,0:T(8,128)} %broadcast_in_dim.31.seg_col, s32[1,3584]{1,0:T(1,128)S(1)} %broadcast_in_dim.29.seg_row, f32[3584,256]{1,0:T(8,128)} %fusion.1.table, bf16[448,384]{1,0:T(8,128)(2,1)S(1)} %copy-done.3, ...), custom_call_target="tpu_custom_call" | custom-call | flops 2348810240 | bytes 11927552 | tf_op jit(solution)/shard_map/attend/pallas_call | solution.py:212
  217.3 1.3 constant_dynamic-slice_fusion
  218.6 1.9 collective-permute-start.39
  220.5 1.6 collective-permute-start.40
  222.1 1.5 collective-permute-start.42
  224.0 4.3 %collective-permute-start.43 = (bf16[448,128]{1,0:T(8,128)(2,1)S(1)}, bf16[448,128]{1,0:T(8,128)(2,1)S(1)}, u32[]{:S(2)}, u32[]{:S(2)}) collective-permute-start(bf16[448,128]{1,0:T(8,128)(2,1)S(1)} %get-tuple-element.85), channel_id=1, source_target_pairs={{0,5},{1,4},{2,1},{3,0},{4,7},{5,6},{6,3},{7,2},{8,13},{9,12},{10,... | collective-permute-start | bytes 344072 | tf_op jit(solution)/shard_map/ppermute | solution.py:412
  228.6 3.1 %collective-permute-start.44 = (bf16[448,128]{1,0:T(8,128)(2,1)S(1)}, bf16[448,128]{1,0:T(8,128)(2,1)S(1)}, u32[]{:S(2)}, u32[]{:S(2)}) collective-permute-start(bf16[448,128]{1,0:T(8,128)(2,1)S(1)} %get-tuple-element.84), channel_id=1, source_target_pairs={{0,7},{1,6},{2,5},{3,4},{4,3},{5,2},{6,1},{7,0},{8,15},{9,14},{10,... | collective-permute-start | bytes 344072 | tf_op jit(solution)/shard_map/ppermute | solution.py:412
  231.7 5.2 %collective-permute-done.41.refs_11_ = bf16[448,128]{1,0:T(8,128)(2,1)S(1)} collective-permute-done((bf16[448,128]{1,0:T(8,128)(2,1)S(1)}, bf16[448,128]{1,0:T(8,128)(2,1)S(1)}, u32[]{:S(2)}, u32[]{:S(2)}) %collective-permute-start.41) | collective-permute-done | bytes 114720 | tf_op jit(solution)/shard_map/ppermute | solution.py:412
  236.9 13.6 %collective-permute-done.42.refs_12_ = bf16[448,128]{1,0:T(8,128)(2,1)S(1)} collective-permute-done((bf16[448,128]{1,0:T(8,128)(2,1)S(1)}, bf16[448,128]{1,0:T(8,128)(2,1)S(1)}, u32[]{:S(2)}, u32[]{:S(2)}) %collective-permute-start.42) | collective-permute-done | bytes 114720 | tf_op jit(solution)/shard_map/ppermute | solution.py:412
  253.9 1.8 collective-permute-done.46.refs_16_
  255.7 1.8 collective-permute-start.49
  258.2 1.8 collective-permute-start.51
  260.6 1.8 collective-permute-start.52
  263.1 1.8 collective-permute-start.53
  265.6 2.5 collective-permute-done.51.refs_21_
  268.1 2.5 collective-permute-done.52.refs_22_
  270.6 2.0 collective-permute-done.53.refs_23_
  294.1 8.2 %project.1 = bf16[448,1024]{1,0:T(8,128)(2,1)} custom-call(s32[3]{0:T(128)S(1)} %pad_add_fusion.where, bf16[448,1024]{1,0:T(8,128)(2,1)S(1)} %copy-done, f32[1,1024]{1,0:T(1,128)S(1)} %bitcast.18, bf16[512,1024]{1,0:T(8,128)(2,1)S(1)} %copy-done.1, bf16[512,1024]{1,0:T(8,128)(2,1)} %collective-permute-done.12.refs_1_, ...), custom_call_target="tpu_custom_call" | custom-call | tf_op jit(solution)/shard_map/project/pallas_call | solution.py:253
  (282 shorter events, 60.7 us)
Async XLA Ops:
  0.0 26.4 %collective-permute-start = (bf16[448,1024]{1,0:T(8,128)(2,1)}, bf16[448,1024]{1,0:T(8,128)(2,1)}, u32[]{:S(2)}, u32[]{:S(2)}) collective-permute-start(bf16[448,1024]{1,0:T(8,128)(2,1)} %tokens.1), channel_id=1, source_target_pairs={{0,4},{1,5},{2,0},{3,1},{4,6},{5,7},{6,2},{7,3},{8,12},{9,13},{10,... | collective-permute-start | bytes 2752520 | tf_op jit(solution)/shard_map/ppermute | solution.py:288
  4.0 22.4 %collective-permute-start.1 = (bf16[448,1024]{1,0:T(8,128)(2,1)}, bf16[448,1024]{1,0:T(8,128)(2,1)}, u32[]{:S(2)}, u32[]{:S(2)}) collective-permute-start(bf16[448,1024]{1,0:T(8,128)(2,1)} %tokens.1), channel_id=1, source_target_pairs={{0,1},{1,0},{2,3},{3,2},{4,5},{5,4},{6,7},{7,6},{8,9},{9,8},{10,11... | collective-permute-start | bytes 2752520 | tf_op jit(solution)/shard_map/ppermute | solution.py:285
  13.7 10.5 %collective-permute-start.2 = (f32[8,448]{1,0:T(8,128)S(1)}, f32[8,448]{1,0:T(8,128)S(1)}, u32[]{:S(2)}, u32[]{:S(2)}) collective-permute-start(f32[8,448]{1,0:T(8,128)S(1)} %maximum_maximum_fusion.stats), channel_id=1, source_target_pairs={{0,4},{1,5},{2,0},{3,1},{4,6},{5,7},{6,2},{7,3},{8,12},{9,13},{10,... | collective-permute-start | bytes 43016 | tf_op jit(solution)/shard_map/ppermute | solution.py:288
  15.3 11.1 %collective-permute-start.3 = (f32[8,448]{1,0:T(8,128)S(1)}, f32[8,448]{1,0:T(8,128)S(1)}, u32[]{:S(2)}, u32[]{:S(2)}) collective-permute-start(f32[8,448]{1,0:T(8,128)S(1)} %maximum_maximum_fusion.stats), channel_id=1, source_target_pairs={{0,1},{1,0},{2,3},{3,2},{4,5},{5,4},{6,7},{7,6},{8,9},{9,8},{10,11... | collective-permute-start | bytes 43016 | tf_op jit(solution)/shard_map/ppermute | solution.py:285
  26.4 23.5 %collective-permute-start.4 = (bf16[448,1024]{1,0:T(8,128)(2,1)}, bf16[448,1024]{1,0:T(8,128)(2,1)}, u32[]{:S(2)}, u32[]{:S(2)}) collective-permute-start(bf16[448,1024]{1,0:T(8,128)(2,1)} %collective-permute-done.own), channel_id=1, source_target_pairs={{0,4},{1,5},{2,0},{3,1},{4,6},{5,7},{6,2},{7,3},{8,12},{9,13},{10,... | collective-permute-start | bytes 2752520 | tf_op jit(solution)/shard_map/ppermute | solution.py:288
  28.1 21.9 %collective-permute-start.5 = (bf16[448,1024]{1,0:T(8,128)(2,1)}, bf16[448,1024]{1,0:T(8,128)(2,1)}, u32[]{:S(2)}, u32[]{:S(2)}) collective-permute-start(bf16[448,1024]{1,0:T(8,128)(2,1)} %collective-permute-done.own), channel_id=1, source_target_pairs={{0,1},{1,0},{2,3},{3,2},{4,5},{5,4},{6,7},{7,6},{8,9},{9,8},{10,11... | collective-permute-start | bytes 2752520 | tf_op jit(solution)/shard_map/ppermute | solution.py:285
  29.6 18.5 %collective-permute-start.6 = (f32[8,448]{1,0:T(8,128)S(1)}, f32[8,448]{1,0:T(8,128)S(1)}, u32[]{:S(2)}, u32[]{:S(2)}) collective-permute-start(f32[8,448]{1,0:T(8,128)S(1)} %collective-permute-done.2.stats), channel_id=1, source_target_pairs={{0,4},{1,5},{2,0},{3,1},{4,6},{5,7},{6,2},{7,3},{8,12},{9,13},{10,... | collective-permute-start | bytes 43016 | tf_op jit(solution)/shard_map/ppermute | solution.py:288
  29.9 19.4 %collective-permute-start.7 = (f32[8,448]{1,0:T(8,128)S(1)}, f32[8,448]{1,0:T(8,128)S(1)}, u32[]{:S(2)}, u32[]{:S(2)}) collective-permute-start(f32[8,448]{1,0:T(8,128)S(1)} %collective-permute-done.2.stats), channel_id=1, source_target_pairs={{0,1},{1,0},{2,3},{3,2},{4,5},{5,4},{6,7},{7,6},{8,9},{9,8},{10,11... | collective-permute-start | bytes 43016 | tf_op jit(solution)/shard_map/ppermute | solution.py:285
  30.4 49.9 %collective-permute-start.19 = (bf16[448,1024]{1,0:T(8,128)(2,1)}, bf16[448,1024]{1,0:T(8,128)(2,1)S(1)}, u32[]{:S(2)}, u32[]{:S(2)}) collective-permute-start(bf16[448,1024]{1,0:T(8,128)(2,1)} %tokens.1), channel_id=1, source_target_pairs={{0,8},{8,0},{16,24},{24,16},{1,9},{9,1},{17,25},{25,17},{2,10},{10... | collective-permute-start | bytes 2752520 | tf_op jit(solution)/shard_map/ppermute | solution.py:291
  49.9 24.8 %collective-permute-start.8 = (bf16[448,1024]{1,0:T(8,128)(2,1)}, bf16[448,1024]{1,0:T(8,128)(2,1)}, u32[]{:S(2)}, u32[]{:S(2)}) collective-permute-start(bf16[448,1024]{1,0:T(8,128)(2,1)} %collective-permute-done.4.own), channel_id=1, source_target_pairs={{0,4},{1,5},{2,0},{3,1},{4,6},{5,7},{6,2},{7,3},{8,12},{9,13},{10,... | collective-permute-start | bytes 2752520 | tf_op jit(solution)/shard_map/ppermute | solution.py:288
  51.1 23.6 %collective-permute-start.9 = (bf16[448,1024]{1,0:T(8,128)(2,1)}, bf16[448,1024]{1,0:T(8,128)(2,1)S(1)}, u32[]{:S(2)}, u32[]{:S(2)}) collective-permute-start(bf16[448,1024]{1,0:T(8,128)(2,1)} %collective-permute-done.4.own), channel_id=1, source_target_pairs={{0,1},{1,0},{2,3},{3,2},{4,5},{5,4},{6,7},{7,6},{8,9},{9,8},{10,11... | collective-permute-start | bytes 2752520 | tf_op jit(solution)/shard_map/ppermute | solution.py:285
  55.0 26.8 %collective-permute-start.21 = (bf16[1024,768]{1,0:T(8,128)(2,1)S(1)}, bf16[1024,768]{1,0:T(8,128)(2,1)S(1)}, u32[]{:S(2)}, u32[]{:S(2)}) collective-permute-start(bf16[1024,768]{1,0:T(8,128)(2,1)S(1)} %pad_maximum_fusion.1), channel_id=1, source_target_pairs={{0,8},{8,0},{16,24},{24,16},{1,9},{9,1},{17,25},{25,17},{2,10},{10... | collective-permute-start | bytes 4718600 | tf_op jit(solution)/shard_map/ppermute | solution.py:291
  55.1 15.3 %collective-permute-start.10 = (f32[8,448]{1,0:T(8,128)S(1)}, f32[8,448]{1,0:T(8,128)S(1)}, u32[]{:S(2)}, u32[]{:S(2)}) collective-permute-start(f32[8,448]{1,0:T(8,128)S(1)} %collective-permute-done.6.stats), channel_id=1, source_target_pairs={{0,4},{1,5},{2,0},{3,1},{4,6},{5,7},{6,2},{7,3},{8,12},{9,13},{10,... | collective-permute-start | bytes 43016 | tf_op jit(solution)/shard_map/ppermute | solution.py:288
  70.4 3.7 %collective-permute-start.11 = (f32[8,448]{1,0:T(8,128)S(1)}, f32[8,448]{1,0:T(8,128)S(1)}, u32[]{:S(2)}, u32[]{:S(2)}) collective-permute-start(f32[8,448]{1,0:T(8,128)S(1)} %collective-permute-done.6.stats), channel_id=1, source_target_pairs={{0,1},{1,0},{2,3},{3,2},{4,5},{5,4},{6,7},{7,6},{8,9},{9,8},{10,11... | collective-permute-start | bytes 43016 | tf_op jit(solution)/shard_map/ppermute | solution.py:285
  74.8 21.5 %collective-permute-start.12 = (bf16[512,1024]{1,0:T(8,128)(2,1)S(1)}, bf16[512,1024]{1,0:T(8,128)(2,1)}, u32[]{:S(2)}, u32[]{:S(2)}) collective-permute-start(bf16[512,1024]{1,0:T(8,128)(2,1)S(1)} %copy-done.1), channel_id=1, source_target_pairs={{0,4},{1,5},{2,0},{3,1},{4,6},{5,7},{6,2},{7,3},{8,12},{9,13},{10,... | collective-permute-start | bytes 3145736 | tf_op jit(solution)/shard_map/ppermute | solution.py:288
  77.4 20.9 %collective-permute-start.13 = (bf16[512,1024]{1,0:T(8,128)(2,1)S(1)}, bf16[512,1024]{1,0:T(8,128)(2,1)S(1)}, u32[]{:S(2)}, u32[]{:S(2)}) collective-permute-start(bf16[512,1024]{1,0:T(8,128)(2,1)S(1)} %copy-done.1), channel_id=1, source_target_pairs={{0,1},{1,0},{2,3},{3,2},{4,5},{5,4},{6,7},{7,6},{8,9},{9,8},{10,11... | collective-permute-start | bytes 3145736 | tf_op jit(solution)/shard_map/ppermute | solution.py:285
  80.2 18.1 %collective-permute-start.22 = (bf16[448,1024]{1,0:T(8,128)(2,1)}, bf16[448,1024]{1,0:T(8,128)(2,1)S(1)}, u32[]{:S(2)}, u32[]{:S(2)}) collective-permute-start(bf16[448,1024]{1,0:T(8,128)(2,1)} %collective-permute-done.own), channel_id=1, source_target_pairs={{0,8},{8,0},{16,24},{24,16},{1,9},{9,1},{17,25},{25,17},{2,10},{10... | collective-permute-start | bytes 2752520 | tf_op jit(solution)/shard_map/ppermute | solution.py:291
  81.2 19.5 %collective-permute-start.25 = (bf16[448,1024]{1,0:T(8,128)(2,1)}, bf16[448,1024]{1,0:T(8,128)(2,1)S(1)}, u32[]{:S(2)}, u32[]{:S(2)}) collective-permute-start(bf16[448,1024]{1,0:T(8,128)(2,1)} %collective-permute-done.1.own), channel_id=1, source_target_pairs={{0,8},{8,0},{16,24},{24,16},{1,9},{9,1},{17,25},{25,17},{2,10},{10... | collective-permute-start | bytes 2752520 | tf_op jit(solution)/shard_map/ppermute | solution.py:291
  86.4 17.9 %collective-permute-start.31 = (bf16[448,384]{1,0:T(8,128)(2,1)}, bf16[448,384]{1,0:T(8,128)(2,1)}, u32[]{:S(2)}, u32[]{:S(2)}) collective-permute-start(bf16[448,384]{1,0:T(8,128)(2,1)} %get-tuple-element.67), channel_id=1, source_target_pairs={{0,16},{8,24},{16,0},{24,8},{1,17},{9,25},{17,1},{25,9},{2,18},{10... | collective-permute-start | bytes 1032200 | tf_op jit(solution)/shard_map/ppermute | solution.py:294
  96.3 10.0 %collective-permute-start.23 = (bf16[448,1024]{1,0:T(8,128)(2,1)}, bf16[448,1024]{1,0:T(8,128)(2,1)}, u32[]{:S(2)}, u32[]{:S(2)}) collective-permute-start(bf16[448,1024]{1,0:T(8,128)(2,1)} %collective-permute-done.4.own), channel_id=1, source_target_pairs={{0,8},{8,0},{16,24},{24,16},{1,9},{9,1},{17,25},{25,17},{2,10},{10... | collective-permute-start | bytes 2752520 | tf_op jit(solution)/shard_map/ppermute | solution.py:291
  98.3 8.0 %collective-permute-start.26 = (bf16[448,1024]{1,0:T(8,128)(2,1)}, bf16[448,1024]{1,0:T(8,128)(2,1)}, u32[]{:S(2)}, u32[]{:S(2)}) collective-permute-start(bf16[448,1024]{1,0:T(8,128)(2,1)} %collective-permute-done.5.own), channel_id=1, source_target_pairs={{0,8},{8,0},{16,24},{24,16},{1,9},{9,1},{17,25},{25,17},{2,10},{10... | collective-permute-start | bytes 2752520 | tf_op jit(solution)/shard_map/ppermute | solution.py:291
  99.2 23.5 %collective-permute-start.28 = (bf16[448,1024]{1,0:T(8,128)(2,1)}, bf16[448,1024]{1,0:T(8,128)(2,1)}, u32[]{:S(2)}, u32[]{:S(2)}) collective-permute-start(bf16[448,1024]{1,0:T(8,128)(2,1)} %collective-permute-done.8.own), channel_id=1, source_target_pairs={{0,1},{1,0},{2,3},{3,2},{4,5},{5,4},{6,7},{7,6},{8,9},{9,8},{10,11... | collective-permute-start | bytes 2752520 | tf_op jit(solution)/shard_map/ppermute | solution.py:285
  101.7 32.2 %collective-permute-start.14 = (bf16[512,1024]{1,0:T(8,128)(2,1)}, bf16[512,1024]{1,0:T(8,128)(2,1)}, u32[]{:S(2)}, u32[]{:S(2)}) collective-permute-start(bf16[512,1024]{1,0:T(8,128)(2,1)} %collective-permute-done.12.refs_1_), channel_id=1, source_target_pairs={{0,4},{1,5},{2,0},{3,1},{4,6},{5,7},{6,2},{7,3},{8,12},{9,13},{10,... | collective-permute-start | bytes 3145736 | tf_op jit(solution)/shard_map/ppermute | solution.py:288
  104.3 40.3 %collective-permute-start.15 = (bf16[512,1024]{1,0:T(8,128)(2,1)}, bf16[512,1024]{1,0:T(8,128)(2,1)S(1)}, u32[]{:S(2)}, u32[]{:S(2)}) collective-permute-start(bf16[512,1024]{1,0:T(8,128)(2,1)} %collective-permute-done.12.refs_1_), channel_id=1, source_target_pairs={{0,1},{1,0},{2,3},{3,2},{4,5},{5,4},{6,7},{7,6},{8,9},{9,8},{10,11... | collective-permute-start | bytes 3145736 | tf_op jit(solution)/shard_map/ppermute | solution.py:285
  106.3 48.9 %collective-permute-start.24 = (bf16[448,1024]{1,0:T(8,128)(2,1)}, bf16[448,1024]{1,0:T(8,128)(2,1)S(1)}, u32[]{:S(2)}, u32[]{:S(2)}) collective-permute-start(bf16[448,1024]{1,0:T(8,128)(2,1)} %collective-permute-done.8.own), channel_id=1, source_target_pairs={{0,8},{8,0},{16,24},{24,16},{1,9},{9,1},{17,25},{25,17},{2,10},{10... | collective-permute-start | bytes 2752520 | tf_op jit(solution)/shard_map/ppermute | solution.py:291
  106.3 47.4 %collective-permute-start.27 = (bf16[448,1024]{1,0:T(8,128)(2,1)}, bf16[448,1024]{1,0:T(8,128)(2,1)S(1)}, u32[]{:S(2)}, u32[]{:S(2)}) collective-permute-start(bf16[448,1024]{1,0:T(8,128)(2,1)} %copy-done.54), channel_id=1, source_target_pairs={{0,8},{8,0},{16,24},{24,16},{1,9},{9,1},{17,25},{25,17},{2,10},{10... | collective-permute-start | bytes 2752520 | tf_op jit(solution)/shard_map/ppermute | solution.py:291
  122.7 33.9 %collective-permute-start.29 = (bf16[448,1024]{1,0:T(8,128)(2,1)}, bf16[448,1024]{1,0:T(8,128)(2,1)S(1)}, u32[]{:S(2)}, u32[]{:S(2)}) collective-permute-start(bf16[448,1024]{1,0:T(8,128)(2,1)} %collective-permute-done.28.own), channel_id=1, source_target_pairs={{0,8},{8,0},{16,24},{24,16},{1,9},{9,1},{17,25},{25,17},{2,10},{10... | collective-permute-start | bytes 2752520 | tf_op jit(solution)/shard_map/ppermute | solution.py:291
  133.9 17.8 %collective-permute-start.32 = (bf16[448,384]{1,0:T(8,128)(2,1)S(1)}, bf16[448,384]{1,0:T(8,128)(2,1)S(1)}, u32[]{:S(2)}, u32[]{:S(2)}) collective-permute-start(bf16[448,384]{1,0:T(8,128)(2,1)S(1)} %get-tuple-element.68), channel_id=1, source_target_pairs={{0,16},{8,24},{16,0},{24,8},{1,17},{9,25},{17,1},{25,9},{2,18},{10... | collective-permute-start | bytes 1032200 | tf_op jit(solution)/shard_map/ppermute | solution.py:294
  145.6 7.5 %collective-permute-start.30 = (f32[8,448]{1,0:T(8,128)S(1)}, f32[8,448]{1,0:T(8,128)S(1)}, u32[]{:S(2)}, u32[]{:S(2)}) collective-permute-start(f32[8,448]{1,0:T(8,128)S(1)} %copy-done.71), channel_id=1, source_target_pairs={{0,1},{1,0},{2,3},{3,2},{4,5},{5,4},{6,7},{7,6},{8,9},{9,8},{10,11... | collective-permute-start | bytes 43016 | tf_op jit(solution)/shard_map/ppermute | solution.py:285
  151.7 17.1 %collective-permute-start.35 = (bf16[448,384]{1,0:T(8,128)(2,1)S(1)}, bf16[448,384]{1,0:T(8,128)(2,1)S(1)}, u32[]{:S(2)}, u32[]{:S(2)}) collective-permute-start(bf16[448,384]{1,0:T(8,128)(2,1)S(1)} %get-tuple-element.71), channel_id=1, source_target_pairs={{0,16},{8,24},{16,0},{24,8},{1,17},{9,25},{17,1},{25,9},{2,18},{10... | collective-permute-start | bytes 1032200 | tf_op jit(solution)/shard_map/ppermute | solution.py:294
  153.2 16.9 %collective-permute-start.33 = (bf16[448,384]{1,0:T(8,128)(2,1)S(1)}, bf16[448,384]{1,0:T(8,128)(2,1)S(1)}, u32[]{:S(2)}, u32[]{:S(2)}) collective-permute-start(bf16[448,384]{1,0:T(8,128)(2,1)S(1)} %get-tuple-element.69), channel_id=1, source_target_pairs={{0,16},{8,24},{16,0},{24,8},{1,17},{9,25},{17,1},{25,9},{2,18},{10... | collective-permute-start | bytes 1032200 | tf_op jit(solution)/shard_map/ppermute | solution.py:294
  153.7 23.7 %collective-permute-start.36 = (bf16[448,384]{1,0:T(8,128)(2,1)S(1)}, bf16[448,384]{1,0:T(8,128)(2,1)S(1)}, u32[]{:S(2)}, u32[]{:S(2)}) collective-permute-start(bf16[448,384]{1,0:T(8,128)(2,1)S(1)} %get-tuple-element.72), channel_id=1, source_target_pairs={{0,16},{8,24},{16,0},{24,8},{1,17},{9,25},{17,1},{25,9},{2,18},{10... | collective-permute-start | bytes 1032200 | tf_op jit(solution)/shard_map/ppermute | solution.py:294
  155.2 61.5 %collective-permute-start.16 = (bf16[512,1024]{1,0:T(8,128)(2,1)}, bf16[512,1024]{1,0:T(8,128)(2,1)}, u32[]{:S(2)}, u32[]{:S(2)}) collective-permute-start(bf16[512,1024]{1,0:T(8,128)(2,1)} %collective-permute-done.14.refs_2_), channel_id=1, source_target_pairs={{0,4},{1,5},{2,0},{3,1},{4,6},{5,7},{6,2},{7,3},{8,12},{9,13},{10,... | collective-permute-start | bytes 3145736 | tf_op jit(solution)/shard_map/ppermute | solution.py:288
  156.6 60.1 %collective-permute-start.17 = (bf16[512,1024]{1,0:T(8,128)(2,1)}, bf16[512,1024]{1,0:T(8,128)(2,1)}, u32[]{:S(2)}, u32[]{:S(2)}) collective-permute-start(bf16[512,1024]{1,0:T(8,128)(2,1)} %collective-permute-done.14.refs_2_), channel_id=1, source_target_pairs={{0,1},{1,0},{2,3},{3,2},{4,5},{5,4},{6,7},{7,6},{8,9},{9,8},{10,11... | collective-permute-start | bytes 3145736 | tf_op jit(solution)/shard_map/ppermute | solution.py:285
  169.5 25.9 %collective-permute-start.37 = (bf16[448,384]{1,0:T(8,128)(2,1)}, bf16[448,384]{1,0:T(8,128)(2,1)S(1)}, u32[]{:S(2)}, u32[]{:S(2)}) collective-permute-start(bf16[448,384]{1,0:T(8,128)(2,1)} %get-tuple-element.73), channel_id=1, source_target_pairs={{0,16},{8,24},{16,0},{24,8},{1,17},{9,25},{17,1},{25,9},{2,18},{10... | collective-permute-start | bytes 1032200 | tf_op jit(solution)/shard_map/ppermute | solution.py:294
  170.8 24.6 %collective-permute-start.34 = (bf16[448,384]{1,0:T(8,128)(2,1)}, bf16[448,384]{1,0:T(8,128)(2,1)S(1)}, u32[]{:S(2)}, u32[]{:S(2)}) collective-permute-start(bf16[448,384]{1,0:T(8,128)(2,1)} %get-tuple-element.70), channel_id=1, source_target_pairs={{0,16},{8,24},{16,0},{24,8},{1,17},{9,25},{17,1},{25,9},{2,18},{10... | collective-permute-start | bytes 1032200 | tf_op jit(solution)/shard_map/ppermute | solution.py:294
  178.1 19.9 %collective-permute-start.38 = (bf16[448,384]{1,0:T(8,128)(2,1)}, bf16[448,384]{1,0:T(8,128)(2,1)S(1)}, u32[]{:S(2)}, u32[]{:S(2)}) collective-permute-start(bf16[448,384]{1,0:T(8,128)(2,1)} %get-tuple-element.74), channel_id=1, source_target_pairs={{0,16},{8,24},{16,0},{24,8},{1,17},{9,25},{17,1},{25,9},{2,18},{10... | collective-permute-start | bytes 1032200 | tf_op jit(solution)/shard_map/ppermute | solution.py:294
  216.7 67.5 %collective-permute-start.18 = (bf16[512,1024]{1,0:T(8,128)(2,1)}, bf16[512,1024]{1,0:T(8,128)(2,1)}, u32[]{:S(2)}, u32[]{:S(2)}) collective-permute-start(bf16[512,1024]{1,0:T(8,128)(2,1)} %collective-permute-done.16.refs_3_), channel_id=1, source_target_pairs={{0,1},{1,0},{2,3},{3,2},{4,5},{5,4},{6,7},{7,6},{8,9},{9,8},{10,11... | collective-permute-start | bytes 3145736 | tf_op jit(solution)/shard_map/ppermute | solution.py:285
  218.6 5.4 %collective-permute-start.39 = (bf16[448,128]{1,0:T(8,128)(2,1)S(1)}, bf16[448,128]{1,0:T(8,128)(2,1)S(1)}, u32[]{:S(2)}, u32[]{:S(2)}) collective-permute-start(bf16[448,128]{1,0:T(8,128)(2,1)S(1)} %get-tuple-element.89), channel_id=1, source_target_pairs={{0,4},{1,5},{2,0},{3,1},{4,6},{5,7},{6,2},{7,3},{8,12},{9,13},{10,... | collective-permute-start | bytes 344072 | tf_op jit(solution)/shard_map/ppermute | solution.py:412
  220.5 8.1 %collective-permute-start.40 = (bf16[448,128]{1,0:T(8,128)(2,1)S(1)}, bf16[448,128]{1,0:T(8,128)(2,1)S(1)}, u32[]{:S(2)}, u32[]{:S(2)}) collective-permute-start(bf16[448,128]{1,0:T(8,128)(2,1)S(1)} %get-tuple-element.88), channel_id=1, source_target_pairs={{0,6},{1,7},{2,4},{3,5},{4,2},{5,3},{6,0},{7,1},{8,14},{9,15},{10,... | collective-permute-start | bytes 344072 | tf_op jit(solution)/shard_map/ppermute | solution.py:412
  222.1 14.8 %collective-permute-start.41 = (bf16[448,128]{1,0:T(8,128)(2,1)S(1)}, bf16[448,128]{1,0:T(8,128)(2,1)S(1)}, u32[]{:S(2)}, u32[]{:S(2)}) collective-permute-start(bf16[448,128]{1,0:T(8,128)(2,1)S(1)} %get-tuple-element.87), channel_id=1, source_target_pairs={{0,2},{1,3},{2,6},{3,7},{4,0},{5,1},{6,4},{7,5},{8,10},{9,11},{10,... | collective-permute-start | bytes 344072 | tf_op jit(solution)/shard_map/ppermute | solution.py:412
  222.1 28.4 %collective-permute-start.42 = (bf16[448,128]{1,0:T(8,128)(2,1)S(1)}, bf16[448,128]{1,0:T(8,128)(2,1)S(1)}, u32[]{:S(2)}, u32[]{:S(2)}) collective-permute-start(bf16[448,128]{1,0:T(8,128)(2,1)S(1)} %get-tuple-element.86), channel_id=1, source_target_pairs={{0,1},{1,0},{2,3},{3,2},{4,5},{5,4},{6,7},{7,6},{8,9},{9,8},{10,11... | collective-permute-start | bytes 344072 | tf_op jit(solution)/shard_map/ppermute | solution.py:412
  224.0 27.8 %collective-permute-start.43 = (bf16[448,128]{1,0:T(8,128)(2,1)S(1)}, bf16[448,128]{1,0:T(8,128)(2,1)S(1)}, u32[]{:S(2)}, u32[]{:S(2)}) collective-permute-start(bf16[448,128]{1,0:T(8,128)(2,1)S(1)} %get-tuple-element.85), channel_id=1, source_target_pairs={{0,5},{1,4},{2,1},{3,0},{4,7},{5,6},{6,3},{7,2},{8,13},{9,12},{10,... | collective-permute-start | bytes 344072 | tf_op jit(solution)/shard_map/ppermute | solution.py:412
  228.6 23.2 %collective-permute-start.44 = (bf16[448,128]{1,0:T(8,128)(2,1)S(1)}, bf16[448,128]{1,0:T(8,128)(2,1)S(1)}, u32[]{:S(2)}, u32[]{:S(2)}) collective-permute-start(bf16[448,128]{1,0:T(8,128)(2,1)S(1)} %get-tuple-element.84), channel_id=1, source_target_pairs={{0,7},{1,6},{2,5},{3,4},{4,3},{5,2},{6,1},{7,0},{8,15},{9,14},{10,... | collective-permute-start | bytes 344072 | tf_op jit(solution)/shard_map/ppermute | solution.py:412
  236.9 15.7 %collective-permute-start.45 = (bf16[448,128]{1,0:T(8,128)(2,1)S(1)}, bf16[448,128]{1,0:T(8,128)(2,1)S(1)}, u32[]{:S(2)}, u32[]{:S(2)}) collective-permute-start(bf16[448,128]{1,0:T(8,128)(2,1)S(1)} %get-tuple-element.83), channel_id=1, source_target_pairs={{0,3},{1,2},{2,7},{3,6},{4,1},{5,0},{6,5},{7,4},{8,11},{9,10},{10,... | collective-permute-start | bytes 344072 | tf_op jit(solution)/shard_map/ppermute | solution.py:412
  250.5 5.2 %collective-permute-start.46 = (bf16[448,128]{1,0:T(8,128)(2,1)S(1)}, bf16[448,128]{1,0:T(8,128)(2,1)S(1)}, u32[]{:S(2)}, u32[]{:S(2)}) collective-permute-start(bf16[448,128]{1,0:T(8,128)(2,1)S(1)} %get-tuple-element.90.refs_8_), channel_id=1, source_target_pairs={{0,16},{8,24},{16,0},{24,8},{1,17},{9,25},{17,1},{25,9},{2,18},{10... | collective-permute-start | bytes 344072 | tf_op jit(solution)/shard_map/ppermute | solution.py:294
  251.8 5.7 %collective-permute-start.54 = (bf16[448,128]{1,0:T(8,128)(2,1)S(1)}, bf16[448,128]{1,0:T(8,128)(2,1)S(1)}, u32[]{:S(2)}, u32[]{:S(2)}) collective-permute-start(bf16[448,128]{1,0:T(8,128)(2,1)S(1)} %get-tuple-element.90.refs_8_), channel_id=1, source_target_pairs={{0,8},{8,0},{16,24},{24,16},{1,9},{9,1},{17,25},{25,17},{2,10},{10... | collective-permute-start | bytes 344072 | tf_op jit(solution)/shard_map/ppermute | solution.py:291
  251.8 6.4 %collective-permute-start.47 = (bf16[448,128]{1,0:T(8,128)(2,1)S(1)}, bf16[448,128]{1,0:T(8,128)(2,1)S(1)}, u32[]{:S(2)}, u32[]{:S(2)}) collective-permute-start(bf16[448,128]{1,0:T(8,128)(2,1)S(1)} %collective-permute-done.39.refs_9_), channel_id=1, source_target_pairs={{0,16},{8,24},{16,0},{24,8},{1,17},{9,25},{17,1},{25,9},{2,18},{10... | collective-permute-start | bytes 344072 | tf_op jit(solution)/shard_map/ppermute | solution.py:294
  252.6 8.0 %collective-permute-start.48 = (bf16[448,128]{1,0:T(8,128)(2,1)S(1)}, bf16[448,128]{1,0:T(8,128)(2,1)S(1)}, u32[]{:S(2)}, u32[]{:S(2)}) collective-permute-start(bf16[448,128]{1,0:T(8,128)(2,1)S(1)} %collective-permute-done.40.refs_10_), channel_id=1, source_target_pairs={{0,16},{8,24},{16,0},{24,8},{1,17},{9,25},{17,1},{25,9},{2,18},{10... | collective-permute-start | bytes 344072 | tf_op jit(solution)/shard_map/ppermute | solution.py:294
  255.7 7.4 %collective-permute-start.49 = (bf16[448,128]{1,0:T(8,128)(2,1)S(1)}, bf16[448,128]{1,0:T(8,128)(2,1)S(1)}, u32[]{:S(2)}, u32[]{:S(2)}) collective-permute-start(bf16[448,128]{1,0:T(8,128)(2,1)S(1)} %collective-permute-done.41.refs_11_), channel_id=1, source_target_pairs={{0,16},{8,24},{16,0},{24,8},{1,17},{9,25},{17,1},{25,9},{2,18},{10... | collective-permute-start | bytes 344072 | tf_op jit(solution)/shard_map/ppermute | solution.py:294
  257.5 8.1 %collective-permute-start.50 = (bf16[448,128]{1,0:T(8,128)(2,1)S(1)}, bf16[448,128]{1,0:T(8,128)(2,1)}, u32[]{:S(2)}, u32[]{:S(2)}) collective-permute-start(bf16[448,128]{1,0:T(8,128)(2,1)S(1)} %collective-permute-done.42.refs_12_), channel_id=1, source_target_pairs={{0,16},{8,24},{16,0},{24,8},{1,17},{9,25},{17,1},{25,9},{2,18},{10... | collective-permute-start | bytes 344072 | tf_op jit(solution)/shard_map/ppermute | solution.py:294
  258.2 9.9 %collective-permute-start.51 = (bf16[448,128]{1,0:T(8,128)(2,1)S(1)}, bf16[448,128]{1,0:T(8,128)(2,1)}, u32[]{:S(2)}, u32[]{:S(2)}) collective-permute-start(bf16[448,128]{1,0:T(8,128)(2,1)S(1)} %collective-permute-done.43.refs_13_), channel_id=1, source_target_pairs={{0,16},{8,24},{16,0},{24,8},{1,17},{9,25},{17,1},{25,9},{2,18},{10... | collective-permute-start | bytes 344072 | tf_op jit(solution)/shard_map/ppermute | solution.py:294
  260.6 9.9 %collective-permute-start.52 = (bf16[448,128]{1,0:T(8,128)(2,1)S(1)}, bf16[448,128]{1,0:T(8,128)(2,1)}, u32[]{:S(2)}, u32[]{:S(2)}) collective-permute-start(bf16[448,128]{1,0:T(8,128)(2,1)S(1)} %collective-permute-done.44.refs_14_), channel_id=1, source_target_pairs={{0,16},{8,24},{16,0},{24,8},{1,17},{9,25},{17,1},{25,9},{2,18},{10... | collective-permute-start | bytes 344072 | tf_op jit(solution)/shard_map/ppermute | solution.py:294
  263.1 9.5 %collective-permute-start.53 = (bf16[448,128]{1,0:T(8,128)(2,1)S(1)}, bf16[448,128]{1,0:T(8,128)(2,1)}, u32[]{:S(2)}, u32[]{:S(2)}) collective-permute-start(bf16[448,128]{1,0:T(8,128)(2,1)S(1)} %collective-permute-done.45.refs_15_), channel_id=1, source_target_pairs={{0,16},{8,24},{16,0},{24,8},{1,17},{9,25},{17,1},{25,9},{2,18},{10... | collective-permute-start | bytes 344072 | tf_op jit(solution)/shard_map/ppermute | solution.py:294
  265.6 7.0 %collective-permute-start.55 = (bf16[448,128]{1,0:T(8,128)(2,1)S(1)}, bf16[448,128]{1,0:T(8,128)(2,1)S(1)}, u32[]{:S(2)}, u32[]{:S(2)}) collective-permute-start(bf16[448,128]{1,0:T(8,128)(2,1)S(1)} %collective-permute-done.39.refs_9_), channel_id=1, source_target_pairs={{0,8},{8,0},{16,24},{24,16},{1,9},{9,1},{17,25},{25,17},{2,10},{10... | collective-permute-start | bytes 344072 | tf_op jit(solution)/shard_map/ppermute | solution.py:291
  268.1 5.7 %collective-permute-start.56 = (bf16[448,128]{1,0:T(8,128)(2,1)S(1)}, bf16[448,128]{1,0:T(8,128)(2,1)S(1)}, u32[]{:S(2)}, u32[]{:S(2)}) collective-permute-start(bf16[448,128]{1,0:T(8,128)(2,1)S(1)} %collective-permute-done.40.refs_10_), channel_id=1, source_target_pairs={{0,8},{8,0},{16,24},{24,16},{1,9},{9,1},{17,25},{25,17},{2,10},{10... | collective-permute-start | bytes 344072 | tf_op jit(solution)/shard_map/ppermute | solution.py:291
  270.6 3.9 %collective-permute-start.57 = (bf16[448,128]{1,0:T(8,128)(2,1)S(1)}, bf16[448,128]{1,0:T(8,128)(2,1)S(1)}, u32[]{:S(2)}, u32[]{:S(2)}) collective-permute-start(bf16[448,128]{1,0:T(8,128)(2,1)S(1)} %collective-permute-done.41.refs_11_), channel_id=1, source_target_pairs={{0,8},{8,0},{16,24},{24,16},{1,9},{9,1},{17,25},{25,17},{2,10},{10... | collective-permute-start | bytes 344072 | tf_op jit(solution)/shard_map/ppermute | solution.py:291
  272.6 3.0 collective-permute-start.58
  273.2 3.0 collective-permute-start.59
  274.4 3.0 collective-permute-start.60
  275.1 3.0 collective-permute-start.61
  276.9 3.0 collective-permute-start.63
  278.1 3.0 collective-permute-start.64
  279.9 3.1 %collective-permute-start.66 = (bf16[448,128]{1,0:T(8,128)(2,1)}, bf16[448,128]{1,0:T(8,128)(2,1)}, u32[]{:S(2)}, u32[]{:S(2)}) collective-permute-start(bf16[448,128]{1,0:T(8,128)(2,1)} %collective-permute-done.50.refs_20_), channel_id=1, source_target_pairs={{0,8},{8,0},{16,24},{24,16},{1,9},{9,1},{17,25},{25,17},{2,10},{10... | collective-permute-start | bytes 344072 | tf_op jit(solution)/shard_map/ppermute | solution.py:291
  (90 other events, 532.2 us)

commit v2 on v1

--- a/solution.py
+++ b/solution.py
@@ -153,112 +153,167 @@
     )(own, peer, stats, affine_own, affine_peer, w_own, w_peer)
 
 
-def attend_kernel(tile, window, blocks, places, lows, seg_col, seg_row, table, *refs):
-    pairs, (out, query, key, value) = refs[: 2 * blocks], refs[2 * blocks :]
-    rows = pairs[0].shape[0]
+def turn_kernel(place, kept, received, table, out, angles, sem):
+    rows = kept.shape[0]
+    at = pl.ds(pl.multiple_of(place[0] * rows, 16), rows)
+    load = pltpu.make_async_copy(table.at[at, :], angles, sem)
+    load.start()
     lane = lax.broadcasted_iota(jnp.int32, (rows, HD), 1)
     first_half = (lane % 64) < 32
+    out[:, 2 * HD :] = (
+        kept[:, 2 * HD :].astype(F32) + received[:, 2 * HD :].astype(F32)
+    ).astype(BF)
+    load.wait()
+    for part in range(2):
+        cols = slice(part * HD, (part + 1) * HD)
+        both = kept[:, cols].astype(F32) + received[:, cols].astype(F32)
+        swapped = jnp.where(first_half, pltpu.roll(both, HD - 32, 1), pltpu.roll(both, 32, 1))
+        out[:, cols] = (both * angles[:, :HD] + swapped * angles[:, HD:]).astype(BF)
+
+
+def turn(place, kept, received, table):
+    rows = kept.shape[0]
+    return pl.pallas_call(
+        turn_kernel,
+        out_shape=jax.ShapeDtypeStruct(kept.shape, BF),
+        in_specs=[whole(pltpu.SMEM), whole(), whole(), whole(pl.ANY)],
+        out_specs=whole(),
+        scratch_shapes=[pltpu.VMEM((rows, 2 * HD), F32), pltpu.SemaphoreType.DMA],
+        compiler_params=pltpu.CompilerParams(vmem_limit_bytes=16 * MIB),
+        cost_estimate=pl.CostEstimate(
+            flops=8 * rows * HD, bytes_accessed=26 * rows * HD, transcendentals=0
+        ),
+        name="turn",
+    )(place, kept, received, table)
+
+
+def attend_kernel(tile, windows, blocks, places, lows, sizes, seg_col, seg_row, *refs):
+    pieces, (out, turned, sems) = refs[:blocks], refs[blocks:]
+    rows = pieces[0].shape[0]
+
+    def load(m):
+        at = pl.ds(pl.multiple_of(places[m] * rows, 16), rows)
+        return pltpu.make_async_copy(pieces[m], turned.at[at, :], sems.at[m])
 
     for m in range(blocks):
-        at = pl.ds(pl.multiple_of(places[m] * rows, 16), rows)
-        cosine = table[at, :HD]
-        sine = table[at, HD:]
-
-        def turned(part):
-            cols = slice(part * HD, (part + 1) * HD)
-            both = pairs[m][:, cols].astype(F32) + pairs[blocks + m][:, cols].astype(F32)
-            if part == 2:
-                return both.astype(BF)
-            swapped = jnp.where(
-                first_half, pltpu.roll(both, HD - 32, 1), pltpu.roll(both, 32, 1)
-            )
-            return (both * cosine + swapped * sine).astype(BF)
-
-        query[at, :] = turned(0)
-        key[at, :] = turned(1)
-        value[at, :] = turned(2)
-
+        load(m).start()
+    for m in range(blocks):
+        load(m).wait()
     scale = HD ** (-0.5) * 1.4426950408889634
 
     def step(i, carry):
         at = pl.ds(pl.multiple_of(i * tile, tile), tile)
-        near = pl.ds(pl.multiple_of(lows[i], 128), window)
-        scores = (
-            lax.dot_general(
-                query[at, :],
-                key[near, :],
-                (((1,), (1,)), ((), ())),
-                preferred_element_type=F32,
+
+        def look(window):
+            near = pl.ds(pl.multiple_of(lows[i], 128), window)
+            scores = (
+                lax.dot_general(
+                    turned[at, :HD],
+                    turned[near, HD : 2 * HD],
+                    (((1,), (1,)), ((), ())),
+                    preferred_element_type=F32,
+                )
+                * scale
             )
-            * scale
-        )
-        marks = seg_col[at, :]
-        scores = jnp.where(marks == seg_row[0:1, near], scores, -1e30)
-        highest = jnp.max(scores, axis=1, keepdims=True)
-        weights = jnp.exp2(scores - highest)
-        total = jnp.sum(weights, axis=1, keepdims=True)
-        result = jnp.dot(weights.astype(BF), value[near, :], preferred_element_type=F32)
-        live = jnp.where(marks >= 0, 1.0 / total, 0.0)
-        out[at, :] = (result * live).astype(BF)
+            marks = seg_col[at, :]
+            scores = jnp.where(marks == seg_row[0:1, near], scores, -1e30)
+            highest = jnp.max(scores, axis=1, keepdims=True)
+            weights = jnp.exp2(scores - highest)
+            total = jnp.sum(weights, axis=1, keepdims=True)
+            result = jnp.dot(
+                weights.astype(BF), turned[near, 2 * HD :], preferred_element_type=F32
+            )
+            live = jnp.where(marks >= 0, 1.0 / total, 0.0)
+            out[at, :] = (result * live).astype(BF)
+
+        for kind, window in enumerate(windows):
+            pl.when(sizes[i] == kind)(functools.partial(look, window))
         return carry
 
     lax.fori_loop(0, out.shape[0] // tile, step, 0)
 
 
-def attend(places, lows, seg_col, seg_row, table, kept, received, tile, window):
-    blocks = len(kept)
+def attend(places, lows, sizes, seg_col, seg_row, pieces, tile, windows):
+    blocks = len(pieces)
     count = seg_col.shape[0]
     smem = whole(pltpu.SMEM)
     return pl.pallas_call(
-        functools.partial(attend_kernel, tile, window, blocks),
+        functools.partial(attend_kernel, tile, windows, blocks),
         out_shape=jax.ShapeDtypeStruct((count, HD), BF),
-        in_specs=[smem, smem] + [whole()] * (3 + 2 * blocks),
+        in_specs=[smem, smem, smem, whole(), whole()] + [whole(pl.ANY)] * blocks,
         out_specs=whole(),
-        scratch_shapes=[pltpu.VMEM((count, HD), BF)] * 3,
-        compiler_params=pltpu.CompilerParams(vmem_limit_bytes=48 * MIB),
+        scratch_shapes=[
+            pltpu.VMEM((count, 3 * HD), BF),
+            pltpu.SemaphoreType.DMA((blocks,)),
+        ],
+        compiler_params=pltpu.CompilerParams(vmem_limit_bytes=32 * MIB),
         cost_estimate=pl.CostEstimate(
-            flops=4 * count * window * HD,
+            flops=4 * count * windows[-1] * HD,
             bytes_accessed=count * HD * 26,
-            transcendentals=count * window,
+            transcendentals=count * windows[-1],
         ),
         name="attend",
-    )(places, lows, seg_col, seg_row, table, *kept, *received)
-
-
-def project_kernel(blocks, where, tokens, layer_scale, *refs):
-    weights = refs[:blocks]
-    parts = refs[blocks : 5 * blocks]
-    out, total = refs[5 * blocks :]
-    even = where[0] == 0
+    )(places, lows, sizes, seg_col, seg_row, *pieces)
+
+
+def project_kernel(blocks, groups, slots, tokens, layer_scale, *refs):
+    weights, parts = refs[:blocks], refs[blocks : blocks + 4 * groups]
+    out, all_weights, rows, weight_sems, sems = refs[blocks + 4 * groups :]
+    depth = weights[0].shape[0]
+    each = blocks // groups
+
+    def load(m):
+        return pltpu.make_async_copy(
+            weights[m], all_weights.at[m * depth : (m + 1) * depth, :], weight_sems.at[m]
+        )
+
+    def place(m, j):
+        start = pl.multiple_of(m * depth + slots[j] * HD, HD)
+        first = (m % each) * HD
+        return pltpu.make_async_copy(
+            parts[4 * (m // each) + j].at[:, first : first + HD],
+            rows.at[:, pl.ds(start, HD)],
+            sems.at[4 * m + j],
+        )
+
     for m in range(blocks):
-        for pair in range(2):
-            one = parts[(2 * pair) * blocks + m][...]
-            two = parts[(2 * pair + 1) * blocks + m][...]
-            rows = jnp.concatenate(
-                [jnp.where(even, one, two), jnp.where(even, two, one)], axis=1
-            )
-            start = pl.multiple_of(where[1 + pair], 2 * HD)
-            term = jnp.dot(
-                rows, weights[m][pl.ds(start, 2 * HD), :], preferred_element_type=F32
-            )
-            if m == 0 and pair == 0:
-                total[...] = term
-            else:
-                total[...] += term
-    out[...] = (tokens[...].astype(F32) + layer_scale[...] * total[...]).astype(BF)
-
-
-def project(where, tokens, layer_scale, weights, parts):
-    blocks = len(weights)
+        load(m).start()
+        for j in range(4):
+            place(m, j).start()
+    for m in range(blocks):
+        load(m).wait()
+        for j in range(4):
+            place(m, j).wait()
+    for start in range(0, out.shape[1], 256):
+        cols = slice(start, start + 256)
+        total = jnp.dot(rows[...], all_weights[:, cols], preferred_element_type=F32)
+        out[:, cols] = (tokens[:, cols].astype(F32) + layer_scale[:, cols] * total).astype(BF)
+
+
+def project(slots, tokens, layer_scale, weights, parts):
+    blocks, groups = len(weights), len(parts) // 4
+    depth = weights[0].shape[0]
+    count, width = tokens.shape
     return pl.pallas_call(
-        functools.partial(project_kernel, blocks),
+        functools.partial(project_kernel, blocks, groups),
         out_shape=jax.ShapeDtypeStruct(tokens.shape, BF),
-        in_specs=[whole(pltpu.SMEM)] + [whole()] * (2 + 5 * blocks),
+        in_specs=[whole(pltpu.SMEM), whole(), whole()]
+        + [whole(pl.ANY)] * (blocks + 4 * groups),
         out_specs=whole(),
-        scratch_shapes=[pltpu.VMEM(tokens.shape, F32)],
-        compiler_params=pltpu.CompilerParams(vmem_limit_bytes=48 * MIB),
+        scratch_shapes=[
+            pltpu.VMEM((blocks * depth, width), BF),
+            pltpu.VMEM((count, blocks * depth), BF),
+            pltpu.SemaphoreType.DMA((blocks,)),
+            pltpu.SemaphoreType.DMA((4 * blocks,)),
+        ],
+        compiler_params=pltpu.CompilerParams(vmem_limit_bytes=32 * MIB),
+        cost_estimate=pl.CostEstimate(
+            flops=2 * count * blocks * depth * width,
+            bytes_accessed=2 * (blocks * depth * (width + count) + 2 * count * width),
+            transcendentals=0,
+        ),
         name="project",
-    )(where, tokens, layer_scale, *weights, *parts)
+    )(slots, tokens, layer_scale, *weights, *parts)
 
 
 def local_heads(
@@ -297,9 +352,9 @@
         return lax.optimization_barrier(values)
 
     source = {}
+    back = {b: a for a, b in after.items()}
     for c in range(cols):
         z, y = c // 2, c % 2
-        back = {b: a for a, b in after.items()}
         for i in range(lines):
             source[c, i] = 2 * z + y
             source[c, lines + i] = 2 * z + 1 - y
@@ -310,6 +365,9 @@
         col
     ]
 
+    z_tok, y_tok = [tokens], []
+    z_new, y_new = by_z(tokens), by_y(tokens)
+
     own_rows = tokens.astype(F32)
     sums = lax.psum(
         jnp.stack([jnp.sum(own_rows, axis=1), jnp.sum(own_rows * own_rows, axis=1)]), "row"
@@ -319,48 +377,21 @@
     own_stats = jnp.concatenate(
         [average[None], lax.rsqrt(spread + 1e-06)[None], jnp.zeros((6, block), F32)]
     )
+    stats = jnp.stack([own_stats, by_y(own_stats)])
+    next_stats = by_z(stats)
 
     width = 3 * HD
 
     def head_columns(which):
         return lax.dynamic_slice_in_dim(w_qkv, which * width, width, 1)
 
+    w_peer = by_core(jnp.concatenate([head_columns(head ^ 2), head_columns(head ^ 3)], axis=1))
     w_own = jnp.concatenate([head_columns(head), head_columns(head ^ 1)], axis=1)
-    w_peer = by_core(jnp.concatenate([head_columns(head ^ 2), head_columns(head ^ 3)], axis=1))
     affine_own = jnp.stack([ln_gain, ln_shift])
     affine_peer = by_core(affine_own)
 
-    def qkv(own, peer, stats):
-        return qkv_block(own, peer, stats, affine_own, affine_peer, w_own, w_peer)
-
-    z_tok, z_stat = [tokens], [own_stats]
-    y_tok, y_stat = [], []
-    for i in range(lines):
-        y_new, y_s = by_y(z_tok[i]), by_y(z_stat[i])
-        if i < lines - 1:
-            z_new, z_s = by_z(z_tok[i]), by_z(z_stat[i])
-            z_new, y_new, z_s, y_s = hold(z_new, y_new, z_s, y_s)
-            z_tok.append(z_new)
-            z_stat.append(z_s)
-        y_tok.append(y_new)
-        y_stat.append(y_s)
-    blocks_tok, blocks_stat = z_tok + y_tok, z_stat + y_stat
-    kept, received = [], []
-    for own, stats in zip(blocks_tok, blocks_stat):
-        keep, send = qkv(own, by_core(own), stats)
-        kept.append(keep)
-        received.append(by_x(send))
-
-    w_first, _ = hold(w_out, z_tok[-1])
-    z_w, y_w = [w_first], []
-    for i in range(lines):
-        y_new = by_y(z_w[i])
-        if i < lines - 1:
-            z_new = by_z(z_w[i])
-            z_new, y_new = hold(z_new, y_new)
-            z_w.append(z_new)
-        y_w.append(y_new)
-    weights = z_w + y_w
+    def qkv(own, peer, its_stats):
+        return qkv_block(own, peer, its_stats, affine_own, affine_peer, w_own, w_peer)
 
     quarter = HD // 4
     frequency = 100.0 ** (-jnp.arange(quarter, dtype=F32) / quarter)
@@ -389,38 +420,89 @@
 
     tile = 256
     reach = -(-(LONGEST - 1) // 128) * 128
-    window = min(count, tile + 2 * reach)
+    windows = tuple(sorted({min(count, w) for w in (512, 640, 896, tile + 2 * reach)}))
     tiles = count // tile
     marks = jnp.where(present == 1, segments, -1)
-    lows = jnp.clip(jnp.arange(tiles, dtype=jnp.int32) * tile - reach, 0, count - window)
-    attended = attend(
-        places,
-        lows,
-        marks[:, None],
-        marks[None, :],
-        table,
-        kept,
-        received,
-        tile,
-        window,
-    )
-
-    parts = []
+    heads_of = segments.reshape(tiles, tile)
+    real = jnp.sum(present)
+    begin = jnp.sum((segments[None, :] < heads_of[:, :1]).astype(jnp.int32), axis=1)
+    end = jnp.sum((segments[None, :] <= heads_of[:, -1:]).astype(jnp.int32), axis=1)
+    begin = jnp.minimum(begin, real) // 128 * 128
+    need = jnp.minimum(end, real) - begin
+    sizes = sum((need > w).astype(jnp.int32) for w in windows[:-1])
+    spans = sum(jnp.where(sizes == k, w, 0) for k, w in enumerate(windows))
+    lows = jnp.minimum(begin, count - spans).astype(jnp.int32)
+    seg_col, seg_row = marks[:, None], marks[None, :]
+
+    own_pair = qkv(tokens, by_core(tokens), stats[0])
+    z_new, y_new, next_stats, table, seg_col, seg_row, lows, sizes, own_keep, own_send = hold(
+        z_new, y_new, next_stats, table, seg_col, seg_row, lows, sizes, *own_pair
+    )
+    kept, sent, received = {0: own_keep}, {0: own_send}, {}
+    ring_stats = [stats]
+    w_ring = [w_out]
+    for i in range(1, lines + 1):
+        y_tok.append(y_new)
+        fresh = [lines + i - 1]
+        if i < lines:
+            z_tok.append(z_new)
+            ring_stats.append(next_stats)
+            fresh.append(i)
+        moving = []
+        if i < lines:
+            y_new = by_y(z_tok[i])
+            moving.append(y_new)
+        if i < lines - 1:
+            z_new, next_stats = by_z(z_tok[i]), by_z(ring_stats[i])
+            moving += [z_new, next_stats]
+        else:
+            w_ring.append(by_z(w_ring[-1]))
+            if i == lines - 1:
+                moving.append(w_ring[-1])
+        for m in list(sent):
+            received[m] = by_x(sent.pop(m))
+        for m in fresh:
+            mine = z_tok[m] if m < lines else y_tok[m - lines]
+            kept[m], sent[m] = qkv(mine, by_core(mine), ring_stats[m % lines][m // lines])
+        if i == lines:
+            break
+        work = [kept[m] for m in fresh] + [sent[m] for m in fresh] + list(received.values())
+        moving = list(hold(*moving, *work))
+        y_new = moving.pop(0)
+        if i < lines - 1:
+            z_new, next_stats = moving.pop(0), moving.pop(0)
+        else:
+            w_ring[-1] = moving.pop(0)
+        for m in fresh:
+            kept[m] = moving.pop(0)
+        for m in fresh:
+            sent[m] = moving.pop(0)
+        for m in received:
+            received[m] = moving.pop(0)
+    for m in list(sent):
+        received[m] = by_x(sent.pop(m))
+    pieces = [turn(places[m : m + 1], kept[m], received[m], table) for m in range(cols)]
+
+    while len(w_ring) < lines:
+        w_ring.append(by_z(w_ring[-1]))
+    weights = w_ring + [by_y(w) for w in w_ring]
+
+    attended = attend(places, lows, sizes, seg_col, seg_row, pieces, tile, windows)
+
+    arrived = []
     for m in range(cols):
         piece = lax.dynamic_slice_in_dim(attended, send_to[m] * block, block, 0)
         pairs = [(c, targets[m][c]) for c in range(cols)]
-        parts.append(piece if m == 0 else lax.ppermute(piece, "col", pairs))
-    x_parts = [by_x(piece) for piece in parts]
-    c_parts = [by_core(piece) for piece in parts]
-    d_parts = [by_core(piece) for piece in x_parts]
-    where = jnp.stack([x_index, core * 2 * HD, (1 - core) * 2 * HD]).astype(jnp.int32)
-    return project(
-        where,
-        tokens,
-        layer_scale[None, :],
-        weights,
-        parts + x_parts + c_parts + d_parts,
-    )
+        arrived.append(piece if m == 0 else lax.ppermute(piece, "col", pairs))
+    half = lines // 2
+    order = [i + lines * y for part in range(2) for y in range(2) for i in range(part * half, (part + 1) * half)]
+    parts = []
+    for part in range(2):
+        group = jnp.concatenate([arrived[m] for m in order[part * lines : (part + 1) * lines]], axis=1)
+        other = by_x(group)
+        parts += [group, other, by_core(group), by_core(other)]
+    slots = jnp.stack([head, head ^ 1, head ^ 2, head ^ 3]).astype(jnp.int32)
+    return project(slots, tokens, layer_scale[None, :], [weights[m] for m in order], parts)
 
 
 def solution(mesh):
@@ -441,7 +523,7 @@
 
     def local(*args):
         heads_here = args[3].shape[1] // (3 * HD)
-        if rows == 4 and heads_here == 4 and cols % 2 == 0 and args[6].shape[0] % 256 == 0:
+        if rows == 4 and heads_here == 4 and cols % 4 == 0 and args[6].shape[0] % 256 == 0:
             return local_heads(*args)
         return local_general(*args)
 

time: 304 us -> 257 us (0.85)
  local copies, waits for them, and re-layouts: 48.2 us -> 20.3 us
  starting transfers between devices: 66 us -> 45 us
  Pallas kernels: 53.2 us -> 63.7 us
  waiting for transfers between devices: 113 us -> 106 us
    unnamed x168 -> x73, local copies, waits for them, and re-layouts: 37.1 us -> 12.9 us
    ppermute x16 -> x10, starting transfers between devices: 20.8 us -> 11.2 us  [by_x(): return lax.ppermute(value, 'row', x_swap)]
    ppermute x7, starting transfers between devices: 12.4 us -> 4.4 us  [local_heads(): arrived.append(piece if m == 0 else lax.ppermute(piece, 'col', pairs))]
    ppermute x7, waiting for transfers between devices: 19.5 us -> 26.2 us  [local_heads(): arrived.append(piece if m == 0 else lax.ppermute(piece, 'col', pairs))]
    ppermute x9, waiting for transfers between devices: 49 us -> 43.4 us  [by_z(): return lax.ppermute(value, 'col', z_next)]
    pallas_call x8, Pallas kernels: 26.4 us -> 31.6 us  [qkv_block(): pl.pallas_call(qkv_kernel, out_shape=(out, out), in_specs=[whole()] * 7,...]
    pallas_call x2 -> x10, Pallas kernels: 26.8 us -> 32.1 us  [the longest x8 13.4 us: turn(): pl.pallas_call(turn_kernel, out_shape=jax.ShapeDtypeStruct(kept.shape, BF...]
    ppermute x12 -> x9, waiting for transfers between devices: 23.5 us -> 18.4 us  [by_y(): return lax.ppermute(value, 'col', y_swap)]
  transfers between devices with their start and end apart: 70 -> 49, of which waited for: 27 -> 17; matrix products, arithmetic and copies ran while one was open for 7% -> 6% of each run, Pallas kernels for 15% -> 22%
where the time goes in v2:
time: 257 us; the launch traced here: 256 us
  waiting for transfers between devices  106 us (41%)
  Pallas kernels  63.7 us (25%)
  starting transfers between devices  45 us (18%)
  local copies, waits for them, and re-layouts  20.3 us (8%)
  blocking collectives  7.44 us (3%)
  between operations  5.94 us (2%)
  other arithmetic  3.79 us (1%)
  matrix products  3.45 us (1%)
    ppermute x9, waiting for transfers between devices, by_z(): return lax.ppermute(value, 'col', z_next)  43.4 us
    pallas_call x8, Pallas kernels, qkv_block(): pl.pallas_call(qkv_kernel, out_shape=(out, out), in_specs=[whole()] * 7,...  31.6 us
    ppermute x7, waiting for transfers between devices, local_heads(): arrived.append(piece if m == 0 else lax.ppermute(piece, 'col', pairs))  26.2 us
    ppermute x9, waiting for transfers between devices, by_y(): return lax.ppermute(value, 'col', y_swap)  18.4 us
    ppermute x9, starting transfers between devices, by_z(): return lax.ppermute(value, 'col', z_next)  16.6 us
    ppermute x10, waiting for transfers between devices, by_x(): return lax.ppermute(value, 'row', x_swap)  15.6 us
    pallas_call x8, Pallas kernels, turn(): pl.pallas_call(turn_kernel, out_shape=jax.ShapeDtypeStruct(kept.shape, BF...  13.4 us
    unnamed x73, local copies, waits for them, and re-layouts  12.9 us
  transfers between devices with their start and end apart: 49, of which 17 were waited for; matrix products, arithmetic and copies ran while one was open for 6% of the time, Pallas kernels for 22%

profile of v2, /device:TPU:0, one launch (start us, length us, event | category | flops | bytes accessed | tf_op | source)
XLA Modules:
  0.0 255.9 jit_solution(14705768852562094555)
XLA Ops:
  0.5 3.6 %collective-permute-start = (bf16[448,1024]{1,0:T(8,128)(2,1)}, bf16[448,1024]{1,0:T(8,128)(2,1)}, u32[]{:S(2)}, u32[]{:S(2)}) collective-permute-start(bf16[448,1024]{1,0:T(8,128)(2,1)} %tokens.1), channel_id=1, source_target_pairs={{0,4},{1,5},{2,0},{3,1},{4,6},{5,7},{6,2},{7,3},{8,12},{9,13},{10,... | collective-permute-start | bytes 2752520 | tf_op jit(solution)/shard_map/ppermute | solution.py:343
  4.0 1.5 collective-permute-start.1
  5.6 3.3 %constant_dynamic-slice_fusion.11 = (bf16[1024,384]{1,0:T(8,128)(2,1)S(1)}, bf16[1024,384]{1,0:T(8,128)(2,1)}, bf16[1024,384]{1,0:T(8,128)(2,1)}, bf16[1024,384]{1,0:T(8,128)(2,1)S(1)}) fusion(bf16[1024,1536]{1,0:T(8,128)(2,1)} %param.15, s32[]{:T(128)S(6)} %select_n.83, s32[]{:T(128)S(6)} %select_n.82, s32[]{:T(128)S(6)} %select_n.81, s32[]{:T(128)S(6)} %select_n.84), kind=kLoop, calls=%fused_computation.51 | loop fusion | bytes 6291472 | tf_op jit(solution)/shard_map/dynamic_slice | solution.py:386
  8.9 1.3 pad_maximum_fusion.1
  10.8 7.4 %psum.7 = f32[2,448]{1,0:T(2,128)S(1)} all-reduce(f32[2,448]{1,0:T(2,128)S(1)} %pad_maximum_fusion.5), channel_id=1, replica_groups=mesh['row'=4,'col'=8] {'row'}, use_global_device_ids=true, to_apply=%region_2.3 | all-reduce | flops 896 | bytes 7168 | tf_op jit(solution)/shard_map/psum | solution.py:372
  19.4 3.5 %fusion.1.table = f32[3584,256]{1,0:T(8,128)} fusion(pred[3584,32]{0,1:T(32,128)(4,1)S(1)} %get-tuple-element.170, pred[3584,32]{0,1:T(32,128)(4,1)S(1)} %get-tuple-element.171, f32[32,256]{1,0:T(8,128)S(1)} %concatenate.34, f32[32,256]{1,0:T(8,128)S(1)} %concatenate.33), kind=kOutput, calls=%fused_computation.5 | convolution fusion | flops 704888832 | bytes 3964928 | tf_op jit(solution)/shard_map/dot_general | solution.py:414
  25.4 1.6 collective-permute-done.2.stats
  27.1 1.2 collective-permute-done.5.affine_peer
  28.3 1.6 collective-permute-start.3
  29.8 4.0 %qkv_block.8 = (bf16[448,384]{1,0:T(8,128)(2,1)S(1)}, bf16[448,384]{1,0:T(8,128)(2,1)S(1)}) custom-call(bf16[448,1024]{1,0:T(8,128)(2,1)S(1)} %copy-done.2, bf16[448,1024]{1,0:T(8,128)(2,1)} %collective-permute-done.4.peer, f32[8,448]{1,0:T(8,128)S(1)} %get-tuple-element.146.stats, f32[2,1024]{1,0:T(2,128)S(1)} %pad_maximum_fusion.4.affine_own, ...), custom_call_target="tpu_custom_call" | custom-call | flops 1409286144 | bytes 5668864 | tf_op jit(solution)/shard_map/qkv_block/pallas_call | solution.py:140
  34.5 1.5 collective-permute-start.7
  36.7 1.5 collective-permute-start.12
  38.3 4.1 %qkv_block.9 = (bf16[448,384]{1,0:T(8,128)(2,1)S(1)}, bf16[448,384]{1,0:T(8,128)(2,1)S(1)}) custom-call(bf16[448,1024]{1,0:T(8,128)(2,1)} %collective-permute-done.1.own, bf16[448,1024]{1,0:T(8,128)(2,1)S(1)} %collective-permute-done.10.peer, f32[8,448]{1,0:T(8,128)S(1)} %collective-permute-done.2.stats, f32[2,1024]{1,0:T(2,128)S(1)} %pad_maximum_fusion.4.affine_own, ...), custom_call_target="tpu_custom_call" | custom-call | flops 1409286144 | bytes 5668864 | tf_op jit(solution)/shard_map/qkv_block/pallas_call | solution.py:140
  43.1 4.0 %qkv_block.10 = (bf16[448,384]{1,0:T(8,128)(2,1)S(1)}, bf16[448,384]{1,0:T(8,128)(2,1)S(1)}) custom-call(bf16[448,1024]{1,0:T(8,128)(2,1)} %collective-permute-done.own, bf16[448,1024]{1,0:T(8,128)(2,1)S(1)} %collective-permute-done.11.peer, f32[8,448]{1,0:T(8,128)S(1)} %get-tuple-element.142.stats, f32[2,1024]{1,0:T(2,128)S(1)} %pad_maximum_fusion.4.affine_own, ...), custom_call_target="tpu_custom_call" | custom-call | flops 1409286144 | bytes 5668864 | tf_op jit(solution)/shard_map/qkv_block/pallas_call | solution.py:140
  47.9 11.1 %collective-permute-done.9 = f32[2,8,448]{2,1,0:T(8,128)S(1)} collective-permute-done((f32[2,8,448]{2,1,0:T(8,128)S(1)}, f32[2,8,448]{2,1,0:T(8,128)S(1)}, u32[]{:S(2)}, u32[]{:S(2)}) %collective-permute-start.9) | collective-permute-done | bytes 28704 | tf_op jit(solution)/shard_map/ppermute | solution.py:343
  60.1 1.6 collective-permute-start.14
  61.6 1.5 collective-permute-start.18
  63.7 3.8 %qkv_block.12 = (bf16[448,384]{1,0:T(8,128)(2,1)S(1)}, bf16[448,384]{1,0:T(8,128)(2,1)S(1)}) custom-call(bf16[448,1024]{1,0:T(8,128)(2,1)S(1)} %collective-permute-done.8.own, bf16[448,1024]{1,0:T(8,128)(2,1)S(1)} %collective-permute-done.17.peer, f32[8,448]{1,0:T(8,128)S(1)} %get-tuple-element.140.stats, f32[2,1024]{1,0:T(2,128)S(1)} %pad_maximum_fusion.4.affine_own, ...), custom_call_target="tpu_custom_call" | custom-call | flops 1409286144 | bytes 5668864 | tf_op jit(solution)/shard_map/qkv_block/pallas_call | solution.py:140
  68.2 0.9 collective-permute-start.15
  69.1 3.8 %qkv_block.11 = (bf16[448,384]{1,0:T(8,128)(2,1)S(1)}, bf16[448,384]{1,0:T(8,128)(2,1)S(1)}) custom-call(bf16[448,1024]{1,0:T(8,128)(2,1)S(1)} %collective-permute-done.7.own, bf16[448,1024]{1,0:T(8,128)(2,1)S(1)} %collective-permute-done.16.peer, f32[8,448]{1,0:T(8,128)S(1)} %get-tuple-element.141.stats, f32[2,1024]{1,0:T(2,128)S(1)} %pad_maximum_fusion.4.affine_own, ...), custom_call_target="tpu_custom_call" | custom-call | flops 1409286144 | bytes 5668864 | tf_op jit(solution)/shard_map/qkv_block/pallas_call | solution.py:140
  73.6 9.2 %collective-permute-done.15 = f32[2,8,448]{2,1,0:T(8,128)S(1)} collective-permute-done((f32[2,8,448]{2,1,0:T(8,128)S(1)}, f32[2,8,448]{2,1,0:T(8,128)S(1)}, u32[]{:S(2)}, u32[]{:S(2)}) %collective-permute-start.15) | collective-permute-done | bytes 28704 | tf_op jit(solution)/shard_map/ppermute | solution.py:343
  83.4 2.5 collective-permute-start.21
  85.9 1.5 collective-permute-start.20
  87.4 1.5 collective-permute-start.24
  89.5 3.8 %qkv_block.14 = (bf16[448,384]{1,0:T(8,128)(2,1)S(1)}, bf16[448,384]{1,0:T(8,128)(2,1)S(1)}) custom-call(bf16[448,1024]{1,0:T(8,128)(2,1)S(1)} %collective-permute-done.14.own, bf16[448,1024]{1,0:T(8,128)(2,1)S(1)} %collective-permute-done.23.peer, f32[8,448]{1,0:T(8,128)S(1)} %get-tuple-element.138.stats, f32[2,1024]{1,0:T(2,128)S(1)} %pad_maximum_fusion.4.affine_own, ...), custom_call_target="tpu_custom_call" | custom-call | flops 1409286144 | bytes 5668864 | tf_op jit(solution)/shard_map/qkv_block/pallas_call | solution.py:140
  94.0 3.9 %qkv_block.13 = (bf16[448,384]{1,0:T(8,128)(2,1)S(1)}, bf16[448,384]{1,0:T(8,128)(2,1)S(1)}) custom-call(bf16[448,1024]{1,0:T(8,128)(2,1)S(1)} %collective-permute-done.13.own, bf16[448,1024]{1,0:T(8,128)(2,1)S(1)} %collective-permute-done.22.peer, f32[8,448]{1,0:T(8,128)S(1)} %get-tuple-element.139.stats, f32[2,1024]{1,0:T(2,128)S(1)} %pad_maximum_fusion.4.affine_own, ...), custom_call_target="tpu_custom_call" | custom-call | flops 1409286144 | bytes 5668864 | tf_op jit(solution)/shard_map/qkv_block/pallas_call | solution.py:140
  97.9 0.8 copy-done.17
  99.4 10.0 %collective-permute-done.21.refs_1_ = bf16[512,1024]{1,0:T(8,128)(2,1)} collective-permute-done((bf16[512,1024]{1,0:T(8,128)(2,1)}, bf16[512,1024]{1,0:T(8,128)(2,1)}, u32[]{:S(2)}, u32[]{:S(2)}) %collective-permute-start.21) | collective-permute-done | bytes 1048608 | tf_op jit(solution)/shard_map/ppermute | solution.py:343
  110.2 0.8 copy-done.19
  110.9 2.9 %collective-permute-start.28 = (bf16[512,1024]{1,0:T(8,128)(2,1)}, bf16[512,1024]{1,0:T(8,128)(2,1)}, u32[]{:S(2)}, u32[]{:S(2)}) collective-permute-start(bf16[512,1024]{1,0:T(8,128)(2,1)} %collective-permute-done.21.refs_1_), channel_id=1, source_target_pairs={{0,4},{1,5},{2,0},{3,1},{4,6},{5,7},{6,2},{7,3},{8,12},{9,13},{10,... | collective-permute-start | bytes 3145736 | tf_op jit(solution)/shard_map/ppermute | solution.py:343
  113.8 1.5 collective-permute-start.26
  115.3 1.5 collective-permute-start.33
  117.3 4.3 %qkv_block.15 = (bf16[448,384]{1,0:T(8,128)(2,1)S(1)}, bf16[448,384]{1,0:T(8,128)(2,1)}) custom-call(bf16[448,1024]{1,0:T(8,128)(2,1)} %collective-permute-done.20.own, bf16[448,1024]{1,0:T(8,128)(2,1)} %collective-permute-done.34.peer, f32[8,448]{1,0:T(8,128)S(1)} %get-tuple-element.137.stats, f32[2,1024]{1,0:T(2,128)S(1)} %pad_maximum_fusion.4.affine_own, ...), custom_call_target="tpu_custom_call" | custom-call | flops 1409286144 | bytes 5668864 | tf_op jit(solution)/shard_map/qkv_block/pallas_call | solution.py:140
  122.4 1.5 collective-permute-start.35
  124.6 13.1 %collective-permute-done.28.refs_4_ = bf16[512,1024]{1,0:T(8,128)(2,1)} collective-permute-done((bf16[512,1024]{1,0:T(8,128)(2,1)}, bf16[512,1024]{1,0:T(8,128)(2,1)}, u32[]{:S(2)}, u32[]{:S(2)}) %collective-permute-start.28) | collective-permute-done | bytes 1048608 | tf_op jit(solution)/shard_map/ppermute | solution.py:343
  137.7 2.9 %collective-permute-start.29 = (bf16[512,1024]{1,0:T(8,128)(2,1)}, bf16[512,1024]{1,0:T(8,128)(2,1)}, u32[]{:S(2)}, u32[]{:S(2)}) collective-permute-start(bf16[512,1024]{1,0:T(8,128)(2,1)} %collective-permute-done.28.refs_4_), channel_id=1, source_target_pairs={{0,4},{1,5},{2,0},{3,1},{4,6},{5,7},{6,2},{7,3},{8,12},{9,13},{10,... | collective-permute-start | bytes 3145736 | tf_op jit(solution)/shard_map/ppermute | solution.py:343
  148.3 2.0 copy-done
  150.3 1.0 copy-done.14
  151.3 1.0 copy-done.22
  152.3 1.3 turn.13.refs_5_
  153.6 1.3 turn.12.refs_4_
  155.0 1.3 turn.10.refs_2_
  156.4 1.4 turn.9.refs_1_
  158.4 1.3 turn.8.refs_0_
  159.7 1.6 collective-permute-start.27
  161.3 2.2 turn.14.refs_6_
  163.6 2.3 turn.11.refs_3_
  165.9 2.2 turn.15.refs_7_
  168.1 10.2 %attend.1 = bf16[3584,128]{1,0:T(8,128)(2,1)S(1)} custom-call(s32[8]{0:T(128)S(1)} %get-tuple-element.148.places, s32[14]{0:T(128)S(1)} %get-tuple-element.93.lows, s32[14]{0:T(128)S(1)} %get-tuple-element.94.sizes, s32[3584,1]{1,0:T(8,128)S(1)} %copy.14.seg_col, s32[1,3584]{1,0:T(1,128)S(1)} %broadcast_in_dim.44.seg_row, bf16[448,384]{1,0:T(8,128)(2,1)S(1)} %turn.8.refs_0_, ...), custom_call_target="tpu_custom_call" | custom-call | flops 2348810240 | bytes 11927552 | tf_op jit(solution)/shard_map/attend/pallas_call | solution.py:240
  178.4 2.2 collective-permute-start.42
  180.6 5.2 %collective-permute-done.42 = bf16[448,128]{1,0:T(8,128)(2,1)S(1)} collective-permute-done((bf16[448,128]{1,0:T(8,128)(2,1)S(1)}, bf16[448,128]{1,0:T(8,128)(2,1)S(1)}, u32[]{:S(2)}, u32[]{:S(2)}) %collective-permute-start.42) | collective-permute-done | bytes 114720 | tf_op jit(solution)/shard_map/ppermute | solution.py:496
  185.9 2.0 collective-permute-start.44
  187.9 1.5 collective-permute-done.43
  189.5 4.0 %collective-permute-done.44 = bf16[448,128]{1,0:T(8,128)(2,1)S(1)} collective-permute-done((bf16[448,128]{1,0:T(8,128)(2,1)S(1)}, bf16[448,128]{1,0:T(8,128)(2,1)S(1)}, u32[]{:S(2)}, u32[]{:S(2)}) %collective-permute-start.44) | collective-permute-done | bytes 114720 | tf_op jit(solution)/shard_map/ppermute | solution.py:496
  193.5 3.9 %collective-permute-done.45 = bf16[448,128]{1,0:T(8,128)(2,1)S(1)} collective-permute-done((bf16[448,128]{1,0:T(8,128)(2,1)S(1)}, bf16[448,128]{1,0:T(8,128)(2,1)S(1)}, u32[]{:S(2)}, u32[]{:S(2)}) %collective-permute-start.45) | collective-permute-done | bytes 114720 | tf_op jit(solution)/shard_map/ppermute | solution.py:496
  198.3 1.2 collective-permute-start.30
  199.5 5.2 %collective-permute-done.37 = bf16[448,128]{1,0:T(8,128)(2,1)S(1)} collective-permute-done((bf16[448,128]{1,0:T(8,128)(2,1)S(1)}, bf16[448,128]{1,0:T(8,128)(2,1)S(1)}, u32[]{:S(2)}, u32[]{:S(2)}) %collective-permute-start.37) | collective-permute-done | bytes 114720 | tf_op jit(solution)/shard_map/ppermute | solution.py:496
  204.8 5.6 %collective-permute-done.38 = bf16[448,128]{1,0:T(8,128)(2,1)S(1)} collective-permute-done((bf16[448,128]{1,0:T(8,128)(2,1)S(1)}, bf16[448,128]{1,0:T(8,128)(2,1)S(1)}, u32[]{:S(2)}, u32[]{:S(2)}) %collective-permute-start.38) | collective-permute-done | bytes 114720 | tf_op jit(solution)/shard_map/ppermute | solution.py:496
  210.5 1.5 collective-permute-start.46
  212.7 9.9 %collective-permute-done.46.refs_13_ = bf16[448,512]{1,0:T(8,128)(2,1)S(1)} collective-permute-done((bf16[448,512]{1,0:T(8,128)(2,1)S(1)}, bf16[448,512]{1,0:T(8,128)(2,1)S(1)}, u32[]{:S(2)}, u32[]{:S(2)}) %collective-permute-start.46) | collective-permute-done | bytes 458784 | tf_op jit(solution)/shard_map/ppermute | solution.py:349
  223.2 5.6 %collective-permute-done.39.refs_9_ = bf16[448,512]{1,0:T(8,128)(2,1)S(1)} collective-permute-done((bf16[448,512]{1,0:T(8,128)(2,1)S(1)}, bf16[448,512]{1,0:T(8,128)(2,1)S(1)}, u32[]{:S(2)}, u32[]{:S(2)}) %collective-permute-start.39) | collective-permute-done | bytes 458784 | tf_op jit(solution)/shard_map/ppermute | solution.py:349
  228.9 1.7 collective-permute-done.41.refs_11_
  230.6 16.7 %collective-permute-done.31.refs_7_ = bf16[512,1024]{1,0:T(8,128)(2,1)S(1)} collective-permute-done((bf16[512,1024]{1,0:T(8,128)(2,1)}, bf16[512,1024]{1,0:T(8,128)(2,1)S(1)}, u32[]{:S(2)}, u32[]{:S(2)}) %collective-permute-start.31) | collective-permute-done | bytes 1048608 | tf_op jit(solution)/shard_map/ppermute | solution.py:340
  247.3 8.5 %project.1 = bf16[448,1024]{1,0:T(8,128)(2,1)} custom-call(s32[4]{0:T(128)S(1)} %pad_add_fusion.slots, bf16[448,1024]{1,0:T(8,128)(2,1)S(1)} %copy-done.2, f32[1,1024]{1,0:T(1,128)S(1)} %bitcast.43, bf16[512,1024]{1,0:T(8,128)(2,1)} %refs_0_.1, bf16[512,1024]{1,0:T(8,128)(2,1)} %collective-permute-done.21.refs_1_, ...), custom_call_target="tpu_custom_call" | custom-call | flops 3758096384 | bytes 13893632 | tf_op jit(solution)/shard_map/project/pallas_call | solution.py:297
  (164 shorter events, 21.9 us)
Async XLA Ops:
  0.0 29.8 %collective-permute-start.4 = (bf16[448,1024]{1,0:T(8,128)(2,1)}, bf16[448,1024]{1,0:T(8,128)(2,1)}, u32[]{:S(2)}, u32[]{:S(2)}) collective-permute-start(bf16[448,1024]{1,0:T(8,128)(2,1)} %tokens.1), channel_id=1, source_target_pairs={{0,8},{8,0},{16,24},{24,16},{1,9},{9,1},{17,25},{25,17},{2,10},{10... | collective-permute-start | bytes 2752520 | tf_op jit(solution)/shard_map/ppermute | solution.py:346
  0.5 33.4 %collective-permute-start = (bf16[448,1024]{1,0:T(8,128)(2,1)}, bf16[448,1024]{1,0:T(8,128)(2,1)}, u32[]{:S(2)}, u32[]{:S(2)}) collective-permute-start(bf16[448,1024]{1,0:T(8,128)(2,1)} %tokens.1), channel_id=1, source_target_pairs={{0,4},{1,5},{2,0},{3,1},{4,6},{5,7},{6,2},{7,3},{8,12},{9,13},{10,... | collective-permute-start | bytes 2752520 | tf_op jit(solution)/shard_map/ppermute | solution.py:343
  4.0 29.9 %collective-permute-start.1 = (bf16[448,1024]{1,0:T(8,128)(2,1)}, bf16[448,1024]{1,0:T(8,128)(2,1)}, u32[]{:S(2)}, u32[]{:S(2)}) collective-permute-start(bf16[448,1024]{1,0:T(8,128)(2,1)} %tokens.1), channel_id=1, source_target_pairs={{0,1},{1,0},{2,3},{3,2},{4,5},{5,4},{6,7},{7,6},{8,9},{9,8},{10,11... | collective-permute-start | bytes 2752520 | tf_op jit(solution)/shard_map/ppermute | solution.py:340
  8.9 1.5 copy-start.2
  8.9 10.0 %copy-start.31 = (s32[2,3584]{1,0:T(2,128)S(1)}, s32[2,3584]{1,0:T(2,128)}, u32[]{:S(2)}) copy-start(s32[2,3584]{1,0:T(2,128)} %param.20) | copy-start | bytes 86020
  10.2 19.7 %collective-permute-start.6 = (bf16[1024,768]{1,0:T(8,128)(2,1)}, bf16[1024,768]{1,0:T(8,128)(2,1)}, u32[]{:S(2)}, u32[]{:S(2)}) collective-permute-start(bf16[1024,768]{1,0:T(8,128)(2,1)} %pad_maximum_fusion.1), channel_id=1, source_target_pairs={{0,8},{8,0},{16,24},{24,16},{1,9},{9,1},{17,25},{25,17},{2,10},{10... | collective-permute-start | bytes 4718600 | tf_op jit(solution)/shard_map/ppermute | solution.py:346
  18.4 8.7 %collective-permute-start.2 = (f32[8,448]{1,0:T(8,128)S(1)}, f32[8,448]{1,0:T(8,128)S(1)}, u32[]{:S(2)}, u32[]{:S(2)}) collective-permute-start(f32[8,448]{1,0:T(8,128)S(1)} %get-tuple-element.146.stats), channel_id=1, source_target_pairs={{0,1},{1,0},{2,3},{3,2},{4,5},{5,4},{6,7},{7,6},{8,9},{9,8},{10,11... | collective-permute-start | bytes 43016 | tf_op jit(solution)/shard_map/ppermute | solution.py:340
  19.4 3.5 %copy-start.28 = (bf16[1024,384]{1,0:T(8,128)(2,1)S(1)}, bf16[1024,384]{1,0:T(8,128)(2,1)}, u32[]{:S(2)}) copy-start(bf16[1024,384]{1,0:T(8,128)(2,1)} %get-tuple-element.126) | copy-start | bytes 2359300
  19.4 3.5 %copy-start.29 = (bf16[1024,384]{1,0:T(8,128)(2,1)S(1)}, bf16[1024,384]{1,0:T(8,128)(2,1)}, u32[]{:S(2)}) copy-start(bf16[1024,384]{1,0:T(8,128)(2,1)} %get-tuple-element.127) | copy-start | bytes 2359300
  22.9 2.5 copy-start.33
  22.9 2.5 copy-start.34
  27.1 1.2 collective-permute-start.5
  28.3 5.6 %collective-permute-start.3 = (f32[2,8,448]{2,1,0:T(8,128)S(1)}, f32[2,8,448]{2,1,0:T(8,128)S(1)}, u32[]{:S(2)}, u32[]{:S(2)}) collective-permute-start(f32[2,8,448]{2,1,0:T(8,128)S(1)} %pad_maximum_fusion.3), channel_id=1, source_target_pairs={{0,4},{1,5},{2,0},{3,1},{4,6},{5,7},{6,2},{7,3},{8,12},{9,13},{10,... | collective-permute-start | bytes 86024 | tf_op jit(solution)/shard_map/ppermute | solution.py:343
  33.9 4.3 %collective-permute-start.10 = (bf16[448,1024]{1,0:T(8,128)(2,1)}, bf16[448,1024]{1,0:T(8,128)(2,1)S(1)}, u32[]{:S(2)}, u32[]{:S(2)}) collective-permute-start(bf16[448,1024]{1,0:T(8,128)(2,1)} %collective-permute-done.1.own), channel_id=1, source_target_pairs={{0,8},{8,0},{16,24},{24,16},{1,9},{9,1},{17,25},{25,17},{2,10},{10... | collective-permute-start | bytes 2752520 | tf_op jit(solution)/shard_map/ppermute | solution.py:346
  34.0 9.1 %collective-permute-start.11 = (bf16[448,1024]{1,0:T(8,128)(2,1)}, bf16[448,1024]{1,0:T(8,128)(2,1)S(1)}, u32[]{:S(2)}, u32[]{:S(2)}) collective-permute-start(bf16[448,1024]{1,0:T(8,128)(2,1)} %collective-permute-done.own), channel_id=1, source_target_pairs={{0,8},{8,0},{16,24},{24,16},{1,9},{9,1},{17,25},{25,17},{2,10},{10... | collective-permute-start | bytes 2752520 | tf_op jit(solution)/shard_map/ppermute | solution.py:346
  34.5 24.5 %collective-permute-start.7 = (bf16[448,1024]{1,0:T(8,128)(2,1)}, bf16[448,1024]{1,0:T(8,128)(2,1)S(1)}, u32[]{:S(2)}, u32[]{:S(2)}) collective-permute-start(bf16[448,1024]{1,0:T(8,128)(2,1)} %collective-permute-done.own), channel_id=1, source_target_pairs={{0,1},{1,0},{2,3},{3,2},{4,5},{5,4},{6,7},{7,6},{8,9},{9,8},{10,11... | collective-permute-start | bytes 2752520 | tf_op jit(solution)/shard_map/ppermute | solution.py:340
  36.0 23.0 %collective-permute-start.8 = (bf16[448,1024]{1,0:T(8,128)(2,1)}, bf16[448,1024]{1,0:T(8,128)(2,1)S(1)}, u32[]{:S(2)}, u32[]{:S(2)}) collective-permute-start(bf16[448,1024]{1,0:T(8,128)(2,1)} %collective-permute-done.own), channel_id=1, source_target_pairs={{0,4},{1,5},{2,0},{3,1},{4,6},{5,7},{6,2},{7,3},{8,12},{9,13},{10,... | collective-permute-start | bytes 2752520 | tf_op jit(solution)/shard_map/ppermute | solution.py:343
  36.7 22.3 %collective-permute-start.12 = (bf16[448,384]{1,0:T(8,128)(2,1)S(1)}, bf16[448,384]{1,0:T(8,128)(2,1)S(1)}, u32[]{:S(2)}, u32[]{:S(2)}) collective-permute-start(bf16[448,384]{1,0:T(8,128)(2,1)S(1)} %get-tuple-element.69), channel_id=1, source_target_pairs={{0,16},{8,24},{16,0},{24,8},{1,17},{9,25},{17,1},{25,9},{2,18},{10... | collective-permute-start | bytes 1032200 | tf_op jit(solution)/shard_map/ppermute | solution.py:349
  38.2 20.8 %collective-permute-start.9 = (f32[2,8,448]{2,1,0:T(8,128)S(1)}, f32[2,8,448]{2,1,0:T(8,128)S(1)}, u32[]{:S(2)}, u32[]{:S(2)}) collective-permute-start(f32[2,8,448]{2,1,0:T(8,128)S(1)} %collective-permute-done.3), channel_id=1, source_target_pairs={{0,4},{1,5},{2,0},{3,1},{4,6},{5,7},{6,2},{7,3},{8,12},{9,13},{10,... | collective-permute-start | bytes 86024 | tf_op jit(solution)/shard_map/ppermute | solution.py:343
  59.0 4.1 %collective-permute-start.17 = (bf16[448,1024]{1,0:T(8,128)(2,1)S(1)}, bf16[448,1024]{1,0:T(8,128)(2,1)S(1)}, u32[]{:S(2)}, u32[]{:S(2)}) collective-permute-start(bf16[448,1024]{1,0:T(8,128)(2,1)S(1)} %collective-permute-done.8.own), channel_id=1, source_target_pairs={{0,8},{8,0},{16,24},{24,16},{1,9},{9,1},{17,25},{25,17},{2,10},{10... | collective-permute-start | bytes 2752520 | tf_op jit(solution)/shard_map/ppermute | solution.py:346
  59.1 9.1 %collective-permute-start.16 = (bf16[448,1024]{1,0:T(8,128)(2,1)S(1)}, bf16[448,1024]{1,0:T(8,128)(2,1)S(1)}, u32[]{:S(2)}, u32[]{:S(2)}) collective-permute-start(bf16[448,1024]{1,0:T(8,128)(2,1)S(1)} %collective-permute-done.7.own), channel_id=1, source_target_pairs={{0,8},{8,0},{16,24},{24,16},{1,9},{9,1},{17,25},{25,17},{2,10},{10... | collective-permute-start | bytes 2752520 | tf_op jit(solution)/shard_map/ppermute | solution.py:346
  59.6 23.3 %collective-permute-start.13 = (bf16[448,1024]{1,0:T(8,128)(2,1)S(1)}, bf16[448,1024]{1,0:T(8,128)(2,1)S(1)}, u32[]{:S(2)}, u32[]{:S(2)}) collective-permute-start(bf16[448,1024]{1,0:T(8,128)(2,1)S(1)} %collective-permute-done.8.own), channel_id=1, source_target_pairs={{0,1},{1,0},{2,3},{3,2},{4,5},{5,4},{6,7},{7,6},{8,9},{9,8},{10,11... | collective-permute-start | bytes 2752520 | tf_op jit(solution)/shard_map/ppermute | solution.py:340
  60.1 22.8 %collective-permute-start.14 = (bf16[448,1024]{1,0:T(8,128)(2,1)S(1)}, bf16[448,1024]{1,0:T(8,128)(2,1)S(1)}, u32[]{:S(2)}, u32[]{:S(2)}) collective-permute-start(bf16[448,1024]{1,0:T(8,128)(2,1)S(1)} %collective-permute-done.8.own), channel_id=1, source_target_pairs={{0,4},{1,5},{2,0},{3,1},{4,6},{5,7},{6,2},{7,3},{8,12},{9,13},{10,... | collective-permute-start | bytes 2752520 | tf_op jit(solution)/shard_map/ppermute | solution.py:343
  61.6 21.2 %collective-permute-start.18 = (bf16[448,384]{1,0:T(8,128)(2,1)S(1)}, bf16[448,384]{1,0:T(8,128)(2,1)S(1)}, u32[]{:S(2)}, u32[]{:S(2)}) collective-permute-start(bf16[448,384]{1,0:T(8,128)(2,1)S(1)} %get-tuple-element.78), channel_id=1, source_target_pairs={{0,16},{8,24},{16,0},{24,8},{1,17},{9,25},{17,1},{25,9},{2,18},{10... | collective-permute-start | bytes 1032200 | tf_op jit(solution)/shard_map/ppermute | solution.py:349
  63.1 19.7 %collective-permute-start.19 = (bf16[448,384]{1,0:T(8,128)(2,1)S(1)}, bf16[448,384]{1,0:T(8,128)(2,1)S(1)}, u32[]{:S(2)}, u32[]{:S(2)}) collective-permute-start(bf16[448,384]{1,0:T(8,128)(2,1)S(1)} %get-tuple-element.79), channel_id=1, source_target_pairs={{0,16},{8,24},{16,0},{24,8},{1,17},{9,25},{17,1},{25,9},{2,18},{10... | collective-permute-start | bytes 1032200 | tf_op jit(solution)/shard_map/ppermute | solution.py:349
  68.2 14.6 %collective-permute-start.15 = (f32[2,8,448]{2,1,0:T(8,128)S(1)}, f32[2,8,448]{2,1,0:T(8,128)S(1)}, u32[]{:S(2)}, u32[]{:S(2)}) collective-permute-start(f32[2,8,448]{2,1,0:T(8,128)S(1)} %collective-permute-done.9), channel_id=1, source_target_pairs={{0,4},{1,5},{2,0},{3,1},{4,6},{5,7},{6,2},{7,3},{8,12},{9,13},{10,... | collective-permute-start | bytes 86024 | tf_op jit(solution)/shard_map/ppermute | solution.py:343
  82.8 10.4 %copy-start.9 = (bf16[448,384]{1,0:T(8,128)(2,1)}, bf16[448,384]{1,0:T(8,128)(2,1)S(1)}, u32[]{:S(2)}) copy-start(bf16[448,384]{1,0:T(8,128)(2,1)S(1)} %collective-permute-done.18.received) | copy-start | bytes 1032196
  82.8 10.4 %copy-start.7 = (bf16[448,384]{1,0:T(8,128)(2,1)}, bf16[448,384]{1,0:T(8,128)(2,1)S(1)}, u32[]{:S(2)}) copy-start(bf16[448,384]{1,0:T(8,128)(2,1)S(1)} %collective-permute-done.19.received) | copy-start | bytes 1032196
  82.9 6.1 %collective-permute-start.23 = (bf16[448,1024]{1,0:T(8,128)(2,1)S(1)}, bf16[448,1024]{1,0:T(8,128)(2,1)S(1)}, u32[]{:S(2)}, u32[]{:S(2)}) collective-permute-start(bf16[448,1024]{1,0:T(8,128)(2,1)S(1)} %collective-permute-done.14.own), channel_id=1, source_target_pairs={{0,8},{8,0},{16,24},{24,16},{1,9},{9,1},{17,25},{25,17},{2,10},{10... | collective-permute-start | bytes 2752520 | tf_op jit(solution)/shard_map/ppermute | solution.py:346
  83.0 11.0 %collective-permute-start.22 = (bf16[448,1024]{1,0:T(8,128)(2,1)S(1)}, bf16[448,1024]{1,0:T(8,128)(2,1)S(1)}, u32[]{:S(2)}, u32[]{:S(2)}) collective-permute-start(bf16[448,1024]{1,0:T(8,128)(2,1)S(1)} %collective-permute-done.13.own), channel_id=1, source_target_pairs={{0,8},{8,0},{16,24},{24,16},{1,9},{9,1},{17,25},{25,17},{2,10},{10... | collective-permute-start | bytes 2752520 | tf_op jit(solution)/shard_map/ppermute | solution.py:346
  83.4 26.0 %collective-permute-start.21 = (bf16[512,1024]{1,0:T(8,128)(2,1)}, bf16[512,1024]{1,0:T(8,128)(2,1)}, u32[]{:S(2)}, u32[]{:S(2)}) collective-permute-start(bf16[512,1024]{1,0:T(8,128)(2,1)} %refs_0_.1), channel_id=1, source_target_pairs={{0,4},{1,5},{2,0},{3,1},{4,6},{5,7},{6,2},{7,3},{8,12},{9,13},{10,... | collective-permute-start | bytes 3145736 | tf_op jit(solution)/shard_map/ppermute | solution.py:343
  85.9 25.0 %collective-permute-start.20 = (bf16[448,1024]{1,0:T(8,128)(2,1)S(1)}, bf16[448,1024]{1,0:T(8,128)(2,1)}, u32[]{:S(2)}, u32[]{:S(2)}) collective-permute-start(bf16[448,1024]{1,0:T(8,128)(2,1)S(1)} %collective-permute-done.14.own), channel_id=1, source_target_pairs={{0,1},{1,0},{2,3},{3,2},{4,5},{5,4},{6,7},{7,6},{8,9},{9,8},{10,11... | collective-permute-start | bytes 2752520 | tf_op jit(solution)/shard_map/ppermute | solution.py:340
  87.4 22.0 %collective-permute-start.24 = (bf16[448,384]{1,0:T(8,128)(2,1)S(1)}, bf16[448,384]{1,0:T(8,128)(2,1)S(1)}, u32[]{:S(2)}, u32[]{:S(2)}) collective-permute-start(bf16[448,384]{1,0:T(8,128)(2,1)S(1)} %get-tuple-element.90), channel_id=1, source_target_pairs={{0,16},{8,24},{16,0},{24,8},{1,17},{9,25},{17,1},{25,9},{2,18},{10... | collective-permute-start | bytes 1032200 | tf_op jit(solution)/shard_map/ppermute | solution.py:349
  88.9 21.2 %collective-permute-start.25 = (bf16[448,384]{1,0:T(8,128)(2,1)S(1)}, bf16[448,384]{1,0:T(8,128)(2,1)S(1)}, u32[]{:S(2)}, u32[]{:S(2)}) collective-permute-start(bf16[448,384]{1,0:T(8,128)(2,1)S(1)} %get-tuple-element.91), channel_id=1, source_target_pairs={{0,16},{8,24},{16,0},{24,8},{1,17},{9,25},{17,1},{25,9},{2,18},{10... | collective-permute-start | bytes 1032200 | tf_op jit(solution)/shard_map/ppermute | solution.py:349
  94.0 3.9 %copy-start.25 = (bf16[448,384]{1,0:T(8,128)(2,1)}, bf16[448,384]{1,0:T(8,128)(2,1)S(1)}, u32[]{:S(2)}) copy-start(bf16[448,384]{1,0:T(8,128)(2,1)S(1)} %get-tuple-element.105) | copy-start | bytes 1032196
  110.9 6.4 %collective-permute-start.34 = (bf16[448,1024]{1,0:T(8,128)(2,1)}, bf16[448,1024]{1,0:T(8,128)(2,1)}, u32[]{:S(2)}, u32[]{:S(2)}) collective-permute-start(bf16[448,1024]{1,0:T(8,128)(2,1)} %collective-permute-done.20.own), channel_id=1, source_target_pairs={{0,8},{8,0},{16,24},{24,16},{1,9},{9,1},{17,25},{25,17},{2,10},{10... | collective-permute-start | bytes 2752520 | tf_op jit(solution)/shard_map/ppermute | solution.py:346
  110.9 26.8 %collective-permute-start.28 = (bf16[512,1024]{1,0:T(8,128)(2,1)}, bf16[512,1024]{1,0:T(8,128)(2,1)}, u32[]{:S(2)}, u32[]{:S(2)}) collective-permute-start(bf16[512,1024]{1,0:T(8,128)(2,1)} %collective-permute-done.21.refs_1_), channel_id=1, source_target_pairs={{0,4},{1,5},{2,0},{3,1},{4,6},{5,7},{6,2},{7,3},{8,12},{9,13},{10,... | collective-permute-start | bytes 3145736 | tf_op jit(solution)/shard_map/ppermute | solution.py:343
  113.8 98.2 %collective-permute-start.26 = (bf16[512,1024]{1,0:T(8,128)(2,1)}, bf16[512,1024]{1,0:T(8,128)(2,1)}, u32[]{:S(2)}, u32[]{:S(2)}) collective-permute-start(bf16[512,1024]{1,0:T(8,128)(2,1)} %refs_0_.1), channel_id=1, source_target_pairs={{0,1},{1,0},{2,3},{3,2},{4,5},{5,4},{6,7},{7,6},{8,9},{9,8},{10,11... | collective-permute-start | bytes 3145736 | tf_op jit(solution)/shard_map/ppermute | solution.py:340
  115.3 44.4 %collective-permute-start.33 = (bf16[448,384]{1,0:T(8,128)(2,1)}, bf16[448,384]{1,0:T(8,128)(2,1)}, u32[]{:S(2)}, u32[]{:S(2)}) collective-permute-start(bf16[448,384]{1,0:T(8,128)(2,1)} %copy-done.26), channel_id=1, source_target_pairs={{0,16},{8,24},{16,0},{24,8},{1,17},{9,25},{17,1},{25,9},{2,18},{10... | collective-permute-start | bytes 1032200 | tf_op jit(solution)/shard_map/ppermute | solution.py:349
  116.8 46.7 %collective-permute-start.32 = (bf16[448,384]{1,0:T(8,128)(2,1)}, bf16[448,384]{1,0:T(8,128)(2,1)}, u32[]{:S(2)}, u32[]{:S(2)}) collective-permute-start(bf16[448,384]{1,0:T(8,128)(2,1)} %copy-done.25), channel_id=1, source_target_pairs={{0,16},{8,24},{16,0},{24,8},{1,17},{9,25},{17,1},{25,9},{2,18},{10... | collective-permute-start | bytes 1032200 | tf_op jit(solution)/shard_map/ppermute | solution.py:349
  122.4 43.5 %collective-permute-start.35 = (bf16[448,384]{1,0:T(8,128)(2,1)}, bf16[448,384]{1,0:T(8,128)(2,1)}, u32[]{:S(2)}, u32[]{:S(2)}) collective-permute-start(bf16[448,384]{1,0:T(8,128)(2,1)} %get-tuple-element.114), channel_id=1, source_target_pairs={{0,16},{8,24},{16,0},{24,8},{1,17},{9,25},{17,1},{25,9},{2,18},{10... | collective-permute-start | bytes 1032200 | tf_op jit(solution)/shard_map/ppermute | solution.py:349
  137.7 67.0 %collective-permute-start.29 = (bf16[512,1024]{1,0:T(8,128)(2,1)}, bf16[512,1024]{1,0:T(8,128)(2,1)}, u32[]{:S(2)}, u32[]{:S(2)}) collective-permute-start(bf16[512,1024]{1,0:T(8,128)(2,1)} %collective-permute-done.28.refs_4_), channel_id=1, source_target_pairs={{0,4},{1,5},{2,0},{3,1},{4,6},{5,7},{6,2},{7,3},{8,12},{9,13},{10,... | collective-permute-start | bytes 3145736 | tf_op jit(solution)/shard_map/ppermute | solution.py:343
  148.3 2.0 copy-start
  156.4 2.0 copy-start.1
  158.4 2.9 %copy-start.18 = (bf16[448,384]{1,0:T(8,128)(2,1)S(1)}, bf16[448,384]{1,0:T(8,128)(2,1)}, u32[]{:S(2)}) copy-start(bf16[448,384]{1,0:T(8,128)(2,1)} %copy-done.17) | copy-start | bytes 1032196
  159.7 52.4 %collective-permute-start.27 = (bf16[512,1024]{1,0:T(8,128)(2,1)}, bf16[512,1024]{1,0:T(8,128)(2,1)S(1)}, u32[]{:S(2)}, u32[]{:S(2)}) collective-permute-start(bf16[512,1024]{1,0:T(8,128)(2,1)} %collective-permute-done.21.refs_1_), channel_id=1, source_target_pairs={{0,1},{1,0},{2,3},{3,2},{4,5},{5,4},{6,7},{7,6},{8,9},{9,8},{10,11... | collective-permute-start | bytes 3145736 | tf_op jit(solution)/shard_map/ppermute | solution.py:340
  161.3 2.2 copy-start.16
  163.5 2.3 copy-start.24
  178.3 69.0 %copy-start.27 = (f32[1024]{0:T(1024)S(1)}, f32[1024]{0:T(1024)}, u32[]{:S(2)}) copy-start(f32[1024]{0:T(1024)} %param.17) | copy-start | bytes 12292
  178.4 7.5 %collective-permute-start.42 = (bf16[448,128]{1,0:T(8,128)(2,1)S(1)}, bf16[448,128]{1,0:T(8,128)(2,1)S(1)}, u32[]{:S(2)}, u32[]{:S(2)}) collective-permute-start(bf16[448,128]{1,0:T(8,128)(2,1)S(1)} %get-tuple-element.132), channel_id=1, source_target_pairs={{0,6},{1,7},{2,4},{3,5},{4,2},{5,3},{6,0},{7,1},{8,14},{9,15},{10,... | collective-permute-start | bytes 344072 | tf_op jit(solution)/shard_map/ppermute | solution.py:496
  180.6 8.9 %collective-permute-start.43 = (bf16[448,128]{1,0:T(8,128)(2,1)S(1)}, bf16[448,128]{1,0:T(8,128)(2,1)S(1)}, u32[]{:S(2)}, u32[]{:S(2)}) collective-permute-start(bf16[448,128]{1,0:T(8,128)(2,1)S(1)} %get-tuple-element.131), channel_id=1, source_target_pairs={{0,2},{1,3},{2,6},{3,7},{4,0},{5,1},{6,4},{7,5},{8,10},{9,11},{10,... | collective-permute-start | bytes 344072 | tf_op jit(solution)/shard_map/ppermute | solution.py:496
  185.9 7.6 %collective-permute-start.44 = (bf16[448,128]{1,0:T(8,128)(2,1)S(1)}, bf16[448,128]{1,0:T(8,128)(2,1)S(1)}, u32[]{:S(2)}, u32[]{:S(2)}) collective-permute-start(bf16[448,128]{1,0:T(8,128)(2,1)S(1)} %get-tuple-element.130), channel_id=1, source_target_pairs={{0,7},{1,6},{2,5},{3,4},{4,3},{5,2},{6,1},{7,0},{8,15},{9,14},{10,... | collective-permute-start | bytes 344072 | tf_op jit(solution)/shard_map/ppermute | solution.py:496
  189.5 7.9 %collective-permute-start.45 = (bf16[448,128]{1,0:T(8,128)(2,1)S(1)}, bf16[448,128]{1,0:T(8,128)(2,1)S(1)}, u32[]{:S(2)}, u32[]{:S(2)}) collective-permute-start(bf16[448,128]{1,0:T(8,128)(2,1)S(1)} %get-tuple-element.129), channel_id=1, source_target_pairs={{0,3},{1,2},{2,7},{3,6},{4,1},{5,0},{6,5},{7,4},{8,11},{9,10},{10,... | collective-permute-start | bytes 344072 | tf_op jit(solution)/shard_map/ppermute | solution.py:496
  193.5 4.8 %collective-permute-start.36 = (bf16[448,128]{1,0:T(8,128)(2,1)S(1)}, bf16[448,128]{1,0:T(8,128)(2,1)S(1)}, u32[]{:S(2)}, u32[]{:S(2)}) collective-permute-start(bf16[448,128]{1,0:T(8,128)(2,1)S(1)} %get-tuple-element.135), channel_id=1, source_target_pairs={{0,4},{1,5},{2,0},{3,1},{4,6},{5,7},{6,2},{7,3},{8,12},{9,13},{10,... | collective-permute-start | bytes 344072 | tf_op jit(solution)/shard_map/ppermute | solution.py:496
  197.3 7.3 %collective-permute-start.37 = (bf16[448,128]{1,0:T(8,128)(2,1)S(1)}, bf16[448,128]{1,0:T(8,128)(2,1)S(1)}, u32[]{:S(2)}, u32[]{:S(2)}) collective-permute-start(bf16[448,128]{1,0:T(8,128)(2,1)S(1)} %get-tuple-element.134), channel_id=1, source_target_pairs={{0,1},{1,0},{2,3},{3,2},{4,5},{5,4},{6,7},{7,6},{8,9},{9,8},{10,11... | collective-permute-start | bytes 344072 | tf_op jit(solution)/shard_map/ppermute | solution.py:496
  198.3 30.6 %collective-permute-start.30 = (bf16[512,1024]{1,0:T(8,128)(2,1)}, bf16[512,1024]{1,0:T(8,128)(2,1)S(1)}, u32[]{:S(2)}, u32[]{:S(2)}) collective-permute-start(bf16[512,1024]{1,0:T(8,128)(2,1)} %collective-permute-done.28.refs_4_), channel_id=1, source_target_pairs={{0,1},{1,0},{2,3},{3,2},{4,5},{5,4},{6,7},{7,6},{8,9},{9,8},{10,11... | collective-permute-start | bytes 3145736 | tf_op jit(solution)/shard_map/ppermute | solution.py:340
  204.7 5.8 %collective-permute-start.38 = (bf16[448,128]{1,0:T(8,128)(2,1)S(1)}, bf16[448,128]{1,0:T(8,128)(2,1)S(1)}, u32[]{:S(2)}, u32[]{:S(2)}) collective-permute-start(bf16[448,128]{1,0:T(8,128)(2,1)S(1)} %get-tuple-element.133), channel_id=1, source_target_pairs={{0,5},{1,4},{2,1},{3,0},{4,7},{5,6},{6,3},{7,2},{8,13},{9,12},{10,... | collective-permute-start | bytes 344072 | tf_op jit(solution)/shard_map/ppermute | solution.py:496
  204.7 42.6 %collective-permute-start.31 = (bf16[512,1024]{1,0:T(8,128)(2,1)}, bf16[512,1024]{1,0:T(8,128)(2,1)S(1)}, u32[]{:S(2)}, u32[]{:S(2)}) collective-permute-start(bf16[512,1024]{1,0:T(8,128)(2,1)} %collective-permute-done.29.refs_5_), channel_id=1, source_target_pairs={{0,1},{1,0},{2,3},{3,2},{4,5},{5,4},{6,7},{7,6},{8,9},{9,8},{10,11... | collective-permute-start | bytes 3145736 | tf_op jit(solution)/shard_map/ppermute | solution.py:340
  210.5 12.2 %collective-permute-start.46 = (bf16[448,512]{1,0:T(8,128)(2,1)S(1)}, bf16[448,512]{1,0:T(8,128)(2,1)S(1)}, u32[]{:S(2)}, u32[]{:S(2)}) collective-permute-start(bf16[448,512]{1,0:T(8,128)(2,1)S(1)} %constant_dynamic-update-slice_fusion.refs_12_), channel_id=1, source_target_pairs={{0,16},{8,24},{16,0},{24,8},{1,17},{9,25},{17,1},{25,9},{2,18},{10... | collective-permute-start | bytes 1376264 | tf_op jit(solution)/shard_map/ppermute | solution.py:349
  212.0 10.7 %collective-permute-start.47 = (bf16[448,512]{1,0:T(8,128)(2,1)S(1)}, bf16[448,512]{1,0:T(8,128)(2,1)S(1)}, u32[]{:S(2)}, u32[]{:S(2)}) collective-permute-start(bf16[448,512]{1,0:T(8,128)(2,1)S(1)} %constant_dynamic-update-slice_fusion.refs_12_), channel_id=1, source_target_pairs={{0,8},{8,0},{16,24},{24,16},{1,9},{9,1},{17,25},{25,17},{2,10},{10... | collective-permute-start | bytes 1376264 | tf_op jit(solution)/shard_map/ppermute | solution.py:346
  212.1 16.7 %collective-permute-start.39 = (bf16[448,512]{1,0:T(8,128)(2,1)S(1)}, bf16[448,512]{1,0:T(8,128)(2,1)S(1)}, u32[]{:S(2)}, u32[]{:S(2)}) collective-permute-start(bf16[448,512]{1,0:T(8,128)(2,1)S(1)} %pad_maximum_fusion.2.refs_8_), channel_id=1, source_target_pairs={{0,16},{8,24},{16,0},{24,8},{1,17},{9,25},{17,1},{25,9},{2,18},{10... | collective-permute-start | bytes 1376264 | tf_op jit(solution)/shard_map/ppermute | solution.py:349
  222.7 6.2 %collective-permute-start.40 = (bf16[448,512]{1,0:T(8,128)(2,1)S(1)}, bf16[448,512]{1,0:T(8,128)(2,1)S(1)}, u32[]{:S(2)}, u32[]{:S(2)}) collective-permute-start(bf16[448,512]{1,0:T(8,128)(2,1)S(1)} %pad_maximum_fusion.2.refs_8_), channel_id=1, source_target_pairs={{0,8},{8,0},{16,24},{24,16},{1,9},{9,1},{17,25},{25,17},{2,10},{10... | collective-permute-start | bytes 1376264 | tf_op jit(solution)/shard_map/ppermute | solution.py:346
  222.7 6.2 %collective-permute-start.48 = (bf16[448,512]{1,0:T(8,128)(2,1)S(1)}, bf16[448,512]{1,0:T(8,128)(2,1)S(1)}, u32[]{:S(2)}, u32[]{:S(2)}) collective-permute-start(bf16[448,512]{1,0:T(8,128)(2,1)S(1)} %collective-permute-done.46.refs_13_), channel_id=1, source_target_pairs={{0,8},{8,0},{16,24},{24,16},{1,9},{9,1},{17,25},{25,17},{2,10},{10... | collective-permute-start | bytes 1376264 | tf_op jit(solution)/shard_map/ppermute | solution.py:346
  228.8 1.8 collective-permute-start.41
  (20 other events, 19.4 us)
